TPU v7x, 32 devices: a whole 2x2x4 slice. The times are simulated.
32 devices in a mesh: groups: 2 (over y), sub: 4 (over z), blk: 2 (over x), rep: 2 (over core).
Axes of the slice: x: 2, y: 2, z: 4, core: 2. Of those that a mesh axis runs over, the one named last changes fastest.
Arguments:
- collocation_locations: float32 [3, 4096], P(None, ('groups', 'sub', 'blk', 'rep')), parts along dimension 1, may hold values from 0 to 8, as said below
- source: float32 [4096], P(('groups', 'sub', 'blk', 'rep')), parts along dimension 0, may hold values from -6 to 6
- propagation_velocity_square: float32 [4096], P(('groups', 'sub', 'blk', 'rep')), parts along dimension 0, may hold values from 0.5 to 2
- live_count: int32 [32], P(('groups', 'sub', 'blk', 'rep')), parts along dimension 0, may hold values from 42 to 128, as said below
- intersection_index: int32 [2, 1024], P(None, ('groups', 'sub', 'blk', 'rep')), parts along dimension 1, may hold values from -1 to 127, as said below
- fine_hidden_matrices: bfloat16 [8, 256, 256], P('sub'), may hold values from -0.375 to 0.375
- fine_edge: bfloat16 [8, 6, 256], P('sub'), may hold values from -4 to 4
- coarse_hidden: bfloat16 [4, 256, 256], P('blk'), may hold values from -0.375 to 0.375
- coarse_edge: bfloat16 [4, 6, 256], P('blk'), may hold values from -4 to 4
Outputs:
- residual: float32 [4096], P(('groups', 'sub', 'blk', 'rep')), parts along dimension 0
- fine_grad_hidden: float32 [16, 256, 256], P(('groups', 'sub')), parts along dimension 0
- fine_grad_edge: float32 [16, 6, 256], P(('groups', 'sub')), parts along dimension 0
- coarse_grad_hidden: float32 [8, 256, 256], P(('groups', 'blk')), parts along dimension 0
- coarse_grad_edge: float32 [8, 6, 256], P(('groups', 'blk')), parts along dimension 0
- mean_loss: float32 [2], P('groups'), parts along dimension 0
There are 2 independent parts, one for each index of `groups`. A program takes and returns all parts, laid end to end along the dimension named above; an argument that names none is the same for every part. Nothing has to cross between parts.
Inputs may be any that keep to these rules, and one draw needn't show every extreme that they name: The first live_count[q] slots of block q hold live points; some block is full. `intersection_index`: for each block, row 0 lists distinct live slots whose points lie in the intersection of the last fine subdomain of the slab on the left (periodically), row 1 those of the first fine subdomain of the slab on the right; used entries come first, then -1; at most 32 used entries per row and block, and some block fills both rows; no slot is in both rows. `collocation_locations`: time and the second space coordinate lie in [0, 1); the first space coordinate of a block of slab s lies in [s * 2, (s + 1) * 2).
All inputs are finite; a program needn't handle non-finite values.
Results may differ from a plain program's by a relative error of at most 0.0033.
Values may be sent and summed in bfloat16 or wider, within the bound.
A program may use at most 64 MiB of HBM per device.

v0:
```python
import jax
import jax.numpy as jnp
from jax import lax
from jax.sharding import PartitionSpec as P

window_width_sq = 0.36
residual_scale = 0.125
fine_factors = (2.0, 2.0, 2.0)


def extended(cells, sides, width):
    for axis, dim in sides:
        count = lax.axis_size(axis)
        head = lax.slice_in_dim(cells, 0, width, axis=dim)
        tail = lax.slice_in_dim(cells, cells.shape[dim] - width, cells.shape[dim], axis=dim)
        cells = jnp.concatenate(
            [
                lax.ppermute(tail, axis, [(i, (i + 1) % count) for i in range(count)]),
                cells,
                lax.ppermute(head, axis, [((i + 1) % count, i) for i in range(count)]),
            ],
            axis=dim,
        )
    return cells


def first_layer(boundary_rows, learner_arguments, unity_multipliers):
    weights_in = boundary_rows[0:3]
    bias_in = boundary_rows[3]
    preact = (
        learner_arguments[0][:, None] * weights_in[0]
        + learner_arguments[1][:, None] * weights_in[1]
        + learner_arguments[2][:, None] * weights_in[2]
        + bias_in
    )
    active = jnp.tanh(preact)
    slopes = 1.0 - active * active
    firsts = [slopes * (unity_multipliers[axis_id] * weights_in[axis_id]) for axis_id in range(3)]
    seconds = [
        -2.0 * active * slopes * (unity_multipliers[axis_id] * weights_in[axis_id]) ** 2
        for axis_id in range(3)
    ]
    return jnp.stack([active] + firsts + seconds)


def second_layer(streams, boundary_rows, unity_bump, wave_speeds):
    bias_mid = boundary_rows[4]
    weights_out = boundary_rows[5] / jnp.sqrt(jnp.float32(boundary_rows.shape[1]))
    active = jnp.tanh(streams[0] + bias_mid)
    slopes = 1.0 - active * active
    net_value = jnp.sum(active * weights_out, axis=-1)
    slope_x = jnp.sum(slopes * streams[2] * weights_out, axis=-1)
    curvature = [
        jnp.sum(
            (slopes * streams[4 + axis_id] - 2.0 * active * slopes * streams[1 + axis_id] ** 2)
            * weights_out,
            axis=-1,
        )
        for axis_id in range(3)
    ]
    weight, weight_x, weight_xx = unity_bump
    return weight * curvature[0] - wave_speeds * (
        weight_xx * net_value
        + 2.0 * weight_x * slope_x
        + weight * curvature[1]
        + weight * curvature[2]
    )


def net_forward(
    hidden_activations, boundary_rows, learner_arguments, unity_multipliers, unity_bump, wave_speeds
):
    streams = first_layer(boundary_rows, learner_arguments, unity_multipliers)
    rounded = streams.astype(jnp.bfloat16)
    rows_total = streams.shape[0] * streams.shape[1]
    columns = streams.shape[2]
    layer_in = jnp.dot(
        rounded.reshape(rows_total, columns), hidden_activations, preferred_element_type=jnp.float32
    ).reshape(streams.shape)
    return (second_layer(layer_in, boundary_rows, unity_bump, wave_speeds), rounded, layer_in)


def net_backward(
    hidden_activations,
    boundary_rows,
    learner_arguments,
    unity_multipliers,
    unity_bump,
    wave_speeds,
    rounded,
    layer_in,
    cotangent,
):
    _, back_out = jax.vjp(
        lambda arg_streams, arg_edges: second_layer(
            arg_streams, arg_edges, unity_bump, wave_speeds
        ),
        layer_in,
        boundary_rows,
    )
    grad_streams, grad_edge_out = back_out(cotangent)
    rows_total = rounded.shape[0] * rounded.shape[1]
    columns = rounded.shape[2]
    grad_low = grad_streams.astype(jnp.bfloat16).reshape(rows_total, columns)
    flat_streams = rounded.reshape(rows_total, columns)
    grad_hidden = lax.dot_general(
        flat_streams, grad_low, (((0,), (0,)), ((), ())), preferred_element_type=jnp.float32
    )
    grad_inputs = lax.dot_general(
        grad_low, hidden_activations, (((1,), (1,)), ((), ())), preferred_element_type=jnp.float32
    ).reshape(rounded.shape)
    _, back_in = jax.vjp(
        lambda arg_edges: first_layer(arg_edges, learner_arguments, unity_multipliers),
        boundary_rows,
    )
    (grad_edge_in,) = back_in(grad_inputs)
    return (grad_hidden, grad_edge_out + grad_edge_in)


def window_of(displacement_amounts, width_sq):
    weight = jnp.exp(-displacement_amounts * displacement_amounts / width_sq)
    weight_x = -2.0 * displacement_amounts / width_sq * weight
    weight_xx = (
        4.0 * displacement_amounts * displacement_amounts / (width_sq * width_sq) - 2.0 / width_sq
    ) * weight
    return (weight, weight_x, weight_xx)


def detailed_level_arrangement(temporal_moments, displacement_amounts, position_vectors):
    learner_arguments = jnp.stack(
        [2.0 * (temporal_moments - 0.5), 2.0 * displacement_amounts, 2.0 * (position_vectors - 0.5)]
    )
    return (learner_arguments, window_of(displacement_amounts, window_width_sq))


def rough_level_arrangement(
    temporal_moments, displacement_amounts, position_vectors, bump_halfwidth
):
    learner_arguments = jnp.stack(
        [
            2.0 * (temporal_moments - 0.5),
            2.0 * displacement_amounts / bump_halfwidth,
            2.0 * (position_vectors - 0.5),
        ]
    )
    unity_multipliers = (2.0, 2.0 / bump_halfwidth, 2.0)
    return (
        learner_arguments,
        window_of(displacement_amounts, window_width_sq * bump_halfwidth * bump_halfwidth),
        unity_multipliers,
    )


def compute_fine_output(
    hidden_activations,
    boundary_rows,
    temporal_moments,
    displacement_amounts,
    position_vectors,
    wave_speeds,
):
    learner_arguments, unity_bump = detailed_level_arrangement(
        temporal_moments, displacement_amounts, position_vectors
    )
    contrib, rounded, layer_in = net_forward(
        hidden_activations, boundary_rows, learner_arguments, fine_factors, unity_bump, wave_speeds
    )
    return (
        contrib,
        (
            hidden_activations,
            boundary_rows,
            learner_arguments,
            fine_factors,
            unity_bump,
            wave_speeds,
            rounded,
            layer_in,
        ),
    )


def backward_stored(stored, cotangent):
    return net_backward(
        stored[0],
        stored[1],
        stored[2],
        stored[3],
        stored[4],
        stored[5],
        stored[6],
        stored[7],
        cotangent,
    )


def shards(
    collocation_locations,
    source,
    propagation_velocity_square,
    live_count,
    intersection_index,
    fine_hidden_matrices,
    fine_edge,
    coarse_hidden,
    coarse_edge,
):
    npoints = collocation_locations.shape[1]
    fine_dev = fine_hidden_matrices.shape[0]
    columns = fine_hidden_matrices.shape[1]
    fine_total = fine_dev * lax.axis_size("sub")
    layer_start_moment = lax.axis_index("sub").astype(jnp.float32) * fine_dev
    positions = jnp.arange(npoints, dtype=jnp.int32)
    live_mask = (positions < live_count[0]).astype(jnp.float32)
    temporal_moments, position_locations, position_vectors = (
        collocation_locations[0],
        collocation_locations[1],
        collocation_locations[2],
    )
    pick_table = (intersection_index[:, :, None] == positions[None, None, :]).astype(jnp.float32)
    fine_boundary_weights = fine_edge.astype(jnp.float32)
    all_coarse = (
        lax.all_gather(coarse_hidden, "blk", axis=0, tiled=True),
        lax.all_gather(coarse_edge, "blk", axis=0, tiled=True),
    )
    all_hidden = all_coarse[0]
    all_edges = all_coarse[1].astype(jnp.float32)
    coarse_total = all_hidden.shape[0]
    slabs_per_cell = lax.axis_size("sub") // coarse_total
    bump_halfwidth = fine_total / coarse_total
    cell_id = lax.axis_index("sub") // slabs_per_cell
    totals = jnp.zeros((npoints,), jnp.float32)
    fine_stored = []
    for piecewise_learner in range(fine_dev):
        displacement_amounts = position_locations - (layer_start_moment + (piecewise_learner + 0.5))
        contrib, stored = compute_fine_output(
            fine_hidden_matrices[piecewise_learner],
            fine_boundary_weights[piecewise_learner],
            temporal_moments,
            displacement_amounts,
            position_vectors,
            propagation_velocity_square,
        )
        totals = totals + contrib
        fine_stored.append(stored)
    coarse_stored = []
    for shift_id in range(3):
        coarse_id = (cell_id + (shift_id - 1)) % coarse_total
        region_centroid = (cell_id.astype(jnp.float32) + (shift_id - 0.5)) * bump_halfwidth
        learner_arguments, unity_bump, unity_multipliers = rough_level_arrangement(
            temporal_moments, position_locations - region_centroid, position_vectors, bump_halfwidth
        )
        net_hidden = all_hidden[coarse_id]
        net_edges = all_edges[coarse_id]
        contrib, rounded, layer_in = net_forward(
            net_hidden,
            net_edges,
            learner_arguments,
            unity_multipliers,
            unity_bump,
            propagation_velocity_square,
        )
        totals = totals + contrib
        coarse_stored.append(
            (
                coarse_id,
                (
                    net_hidden,
                    net_edges,
                    learner_arguments,
                    unity_multipliers,
                    unity_bump,
                    propagation_velocity_square,
                    rounded,
                    layer_in,
                ),
            )
        )
    centers = jnp.stack([layer_start_moment - 0.5, layer_start_moment + (fine_dev + 0.5)])
    field_values = jnp.stack(
        [temporal_moments, position_locations, position_vectors, propagation_velocity_square]
    )
    gathered = jnp.einsum("rcp,fp->frc", pick_table, field_values, precision=lax.Precision.HIGHEST)
    listed = jnp.stack([gathered[0], gathered[1] - centers[:, None], gathered[2], gathered[3]])
    packed = jnp.concatenate([fine_hidden_matrices, fine_edge], axis=1)
    beside_all = extended(packed, (("sub", 0),), 1)
    left_net = beside_all[0]
    right_net = beside_all[beside_all.shape[0] - 1]
    left_values, left_stored = compute_fine_output(
        left_net[:columns],
        left_net[columns:].astype(jnp.float32),
        listed[0, 0],
        listed[1, 0],
        listed[2, 0],
        listed[3, 0],
    )
    right_values, right_stored = compute_fine_output(
        right_net[:columns],
        right_net[columns:].astype(jnp.float32),
        listed[0, 1],
        listed[1, 1],
        listed[2, 1],
        listed[3, 1],
    )
    remote_values = jnp.stack([left_values, right_values])
    totals = totals + jnp.einsum(
        "rc,rcp->p", remote_values, pick_table, precision=lax.Precision.HIGHEST
    )
    residual = (totals * residual_scale - source) * live_mask
    loss_parts = lax.psum(
        (jnp.sum(residual * residual), live_count[0].astype(jnp.float32)), ("sub", "blk", "rep")
    )
    mean_loss = (loss_parts[0] / loss_parts[1]).reshape(1)
    cotangent = residual * residual_scale
    grads_hidden = []
    grads_edge = []
    for piecewise_learner in range(fine_dev):
        grad_hidden, grad_edges = backward_stored(fine_stored[piecewise_learner], cotangent)
        grads_hidden.append(grad_hidden)
        grads_edge.append(grad_edges)
    listed_cotangent = jnp.einsum(
        "rcp,p->rc", pick_table, cotangent, precision=lax.Precision.HIGHEST
    )
    left_hidden, left_edges = backward_stored(left_stored, listed_cotangent[0])
    right_hidden, right_edges = backward_stored(right_stored, listed_cotangent[1])
    outgoing_grads = jnp.stack(
        [
            jnp.concatenate([left_hidden, left_edges], axis=0),
            jnp.concatenate([right_hidden, right_edges], axis=0),
        ]
    )
    returned = extended(outgoing_grads.astype(jnp.bfloat16), (("sub", 0),), 1).astype(
        outgoing_grads.dtype
    )
    first_grads = returned[0]
    last_grads = returned[returned.shape[0] - 1]
    grads_hidden[0] = grads_hidden[0] + first_grads[:columns]
    grads_edge[0] = grads_edge[0] + first_grads[columns:]
    grads_hidden[fine_dev - 1] = grads_hidden[fine_dev - 1] + last_grads[:columns]
    grads_edge[fine_dev - 1] = grads_edge[fine_dev - 1] + last_grads[columns:]
    coarse_buffer_hidden = jnp.zeros((coarse_total, columns, columns), jnp.float32)
    coarse_buffer_edge = jnp.zeros((coarse_total, 6, columns), jnp.float32)
    for coarse_id, stored in coarse_stored:
        grad_hidden, grad_edges = backward_stored(stored, cotangent)
        coarse_buffer_hidden = coarse_buffer_hidden.at[coarse_id].add(grad_hidden)
        coarse_buffer_edge = coarse_buffer_edge.at[coarse_id].add(grad_edges)
    fine_gh = jnp.stack(grads_hidden)
    fine_ge = jnp.stack(grads_edge)
    fine_sums = lax.psum((fine_gh, fine_ge), ("blk", "rep"))
    owned = (
        lax.psum_scatter(coarse_buffer_hidden, "blk", scatter_dimension=0, tiled=True),
        lax.psum_scatter(coarse_buffer_edge, "blk", scatter_dimension=0, tiled=True),
    )
    coarse_sums = lax.psum((owned[0], owned[1]), ("sub", "rep"))
    return (residual, fine_sums[0], fine_sums[1], coarse_sums[0], coarse_sums[1], mean_loss)


def solution(mesh):
    return jax.shard_map(
        shards,
        mesh=mesh,
        in_specs=(
            P(None, ("groups", "sub", "blk", "rep")),
            P(("groups", "sub", "blk", "rep")),
            P(("groups", "sub", "blk", "rep")),
            P(("groups", "sub", "blk", "rep")),
            P(None, ("groups", "sub", "blk", "rep")),
            P("sub", None, None),
            P("sub", None, None),
            P("blk", None, None),
            P("blk", None, None),
        ),
        out_specs=(
            P(("groups", "sub", "blk", "rep")),
            P(("groups", "sub"), None, None),
            P(("groups", "sub"), None, None),
            P(("groups", "blk"), None, None),
            P(("groups", "blk"), None, None),
            P("groups"),
        ),
        check_vma=False,
    )
```

profile of v0, /device:TPU:0, one launch (start us, length us, event | category | flops | bytes accessed | tf_op | source)
XLA Modules:
  0.0 237.8 jit_solution(3869574930918475308)
XLA Ops:
  8.1 1.0 constant_dynamic-update-slice_fusion.36
  9.1 0.7 fusion.462
  9.8 3.0 %collective-permute-start = (bf16[1,262,256]{2,1,0:T(8,128)(2,1)}, bf16[1,262,256]{2,1,0:T(8,128)(2,1)}, u32[]{:S(2)}, u32[]{:S(2)}) collective-permute-start(bf16[1,262,256]{2,1,0:T(8,128)(2,1)} %get-tuple-element.370), channel_id=1, source_target_pairs={{0,4},{4,8},{8,12},{12,0},{1,5},{5,9},{9,13},{13,1},{2,6},{6,10},{... | collective-permute-start | bytes 402440 | tf_op jit(solution)/shard_map/ppermute | solution.py:18
  12.8 2.0 collective-permute-start.1
  17.1 4.4 %all_gather.6 = bf16[4,6,256]{2,1,0:T(8,128)(2,1)S(1)} all-gather(bf16[2,6,256]{2,1,0:T(8,128)(2,1)S(1)} %copy.31), channel_id=1, replica_groups=mesh['groups'=2,'sub'=4,'blk'=2,'rep'=2] {'blk'}, dimensions={0}, use_global_device_ids=true | all-gather | bytes 18432 | tf_op jit(solution)/shard_map/all_gather | solution.py:224
  27.1 1.1 constant_dynamic-update-slice_fusion.11
  28.8 1.2 constant_dynamic-update-slice_fusion.10
  30.6 1.2 constant_dynamic-update-slice_fusion.6
  31.8 0.8 copy-done.14
  32.9 0.7 copy-done.29
  33.6 7.8 %all_gather.7 = bf16[4,256,256]{2,1,0:T(8,128)(2,1)S(1)} all-gather(bf16[2,256,256]{2,1,0:T(8,128)(2,1)S(1)} %copy-done.29), channel_id=1, replica_groups=mesh['groups'=2,'sub'=4,'blk'=2,'rep'=2] {'blk'}, dimensions={0}, use_global_device_ids=true | all-gather | bytes 786432 | tf_op jit(solution)/shard_map/all_gather | solution.py:223
  41.4 1.5 constant_dynamic-update-slice_fusion.19
  42.9 0.8 constant_dynamic-update-slice_fusion.18
  43.8 1.0 constant_dynamic-update-slice_fusion.17
  44.8 1.1 constant_dynamic-update-slice_fusion.16
  46.2 1.8 constant_dynamic-update-slice_fusion.5
  48.0 1.7 constant_dynamic-update-slice_fusion.4
  49.7 1.0 copy.33
  51.0 0.7 copy-done.16
  52.8 1.7 constant_dynamic-update-slice_fusion.3
  54.5 1.7 constant_dynamic-update-slice_fusion.2
  56.2 1.2 copy.32
  57.5 1.2 fusion.144
  59.4 1.8 constant_dynamic-update-slice_fusion.1
  61.1 1.8 constant_dynamic-update-slice_fusion
  64.3 1.2 copy.29
  66.5 1.4 multiply_reduce_fusion.73
  67.9 1.5 multiply_reduce_fusion.78
  70.1 0.8 multiply_reduce_fusion.83
  71.5 1.5 multiply_reduce_fusion.88
  73.7 1.4 multiply_reduce_fusion.93
  77.0 0.8 and_reduce_fusion
  81.9 1.1 fusion.200
  83.1 1.1 fusion.202
  87.2 1.1 fusion.199
  89.2 1.7 collective-permute-start.3
  91.5 1.1 fusion.201
  93.9 1.2 multiply_reduce_fusion.133
  95.8 0.9 multiply_bitcast_fusion.9
  96.8 0.8 multiply_reduce_fusion.68
  97.6 1.3 fusion.150
  100.2 1.1 broadcast_in_dim.148
  101.3 2.7 %fusion.8 = f32[4,256,256]{2,1,0:T(8,128)} fusion(f32[4,256,256]{2,1,0:T(8,128)} %broadcast_in_dim.148, s32[]{:T(128)} %select_n.42, bf16[7,128,256]{1,2,0:T(8,128)(2,1)} %get-tuple-element.505, bf16[7,128,256]{2,1,0:T(8,128)(2,1)S(1)} %add_convert_fusion.2, pred[]{:T(512)} %get-tuple-element.594), kind=kOutput, calls=%fused_computation.15 | convolution fusion | flops 117506048 | bytes 1180672 | tf_op jit(solution)/shard_map/dot_general | solution.py:106
  106.0 1.0 copy-done.13
  106.9 2.6 %fusion.2 = f32[4,256,256]{2,1,0:T(8,128)} fusion(f32[4,256,256]{2,1,0:T(8,128)} %fusion.8, s32[]{:T(128)} %select_n.44, bf16[7,128,256]{1,2,0:T(8,128)(2,1)S(1)} %copy-done.13, bf16[7,128,256]{2,1,0:T(8,128)(2,1)S(1)} %add_convert_fusion.1, pred[]{:T(512)} %get-tuple-element.264), kind=kOutput, calls=%fused_computation.7 | convolution fusion | flops 117571584 | bytes 1442816 | tf_op jit(solution)/shard_map/dot_general | solution.py:106
  111.3 0.8 multiply_reduce_fusion.12
  112.1 1.0 copy-done.15
  113.0 2.6 %fusion.5 = f32[4,256,256]{2,1,0:T(8,128)} fusion(f32[4,256,256]{2,1,0:T(8,128)} %fusion.2, s32[]{:T(128)} %select_n.46, bf16[7,128,256]{1,2,0:T(8,128)(2,1)S(1)} %copy-done.15, bf16[7,128,256]{2,1,0:T(8,128)(2,1)S(1)} %add_convert_fusion, pred[]{:T(512)} %get-tuple-element.263), kind=kOutput, calls=%fused_computation.10 | convolution fusion | flops 117571584 | bytes 1442816 | tf_op jit(solution)/shard_map/dot_general | solution.py:106
  115.9 1.2 fusion.142
  117.2 1.1 fusion.443
  122.7 0.8 bitcast_dynamic-update-slice_fusion
  123.5 0.7 fusion.282
  125.7 1.1 fusion.444
  127.6 1.1 fusion.445
  129.5 0.8 fusion.309
  131.4 1.5 fusion.18
  132.8 0.8 pad_maximum_fusion
  133.8 3.6 %reduce-scatter.3.cloned.1.call-done = f32[2,256,256]{2,1,0:T(8,128)} async-done(((f32[4,256,256]{2,1,0:T(8,128)}), f32[2,256,256]{2,1,0:T(8,128)}) %reduce-scatter.3.cloned.1.call-update) | async-done | bytes 524304 | tf_op jit(solution)/shard_map/reduce_scatter | solution.py:351
  137.4 32.8 %all-reduce.147 = (f32[]{:T(128)}, f32[]{:T(128)}) all-reduce(f32[]{:T(128)} %get-tuple-element.557, f32[]{:T(128)S(6)} %convert_element_type.147), channel_id=1, replica_groups=mesh['groups'=2,'sub'=4,'blk'=2,'rep'=2] {'sub','blk','rep'}, use_global_device_ids=true, to_apply=%region_157.158 | all-reduce | flops 2 | bytes 16 | tf_op jit(solution)/shard_map/psum | solution.py:310
  171.6 26.6 %psum.45 = f32[2,6,256]{2,1,0:T(8,128)S(1)} all-reduce(f32[2,6,256]{2,1,0:T(8,128)} %reduce-scatter.5.cloned.1.call-done), channel_id=1, replica_groups=mesh['groups'=2,'sub'=4,'blk'=2,'rep'=2] {'sub','rep'}, use_global_device_ids=true, to_apply=%region_155.156 | all-reduce | flops 3072 | bytes 24576 | tf_op jit(solution)/shard_map/psum | solution.py:354
  200.2 10.5 %psum.43 = f32[2,6,256]{2,1,0:T(8,128)S(1)} all-reduce(f32[2,6,256]{2,1,0:T(8,128)S(1)} %pad_maximum_fusion.1), channel_id=1, replica_groups=mesh['groups'=2,'sub'=4,'blk'=2,'rep'=2] {'blk','rep'}, use_global_device_ids=true, to_apply=%region_100.101 | all-reduce | flops 3072 | bytes 24576 | tf_op jit(solution)/shard_map/psum | solution.py:349
  211.4 15.2 %all-reduce.153.cloned.1.call-done = f32[2,256,256]{2,1,0:T(8,128)} async-done(((f32[2,256,256]{2,1,0:T(8,128)}), f32[2,256,256]{2,1,0:T(8,128)}) %all-reduce.153.cloned.1.call-update) | async-done | bytes 524304 | tf_op jit(solution)/shard_map/psum | solution.py:354
  226.6 1.9 copy.94
  228.5 0.8 copy.95
  (566 shorter events, 42.5 us)
Async XLA Ops:
  8.0 129.4 %reduce-scatter.3.cloned.1.call-start = ((), (), s32[]{:S(2)}) async-start(), calls=%async_computation.3 | async-start | bytes 1572864 | tf_op jit(solution)/shard_map/reduce_scatter | solution.py:351
  9.0 12.4 %copy-start.79 = (f32[2,6,256]{2,1,0:T(8,128)}, f32[2,6,256]{2,1,0:T(8,128)S(1)}, u32[]{:S(2)}) copy-start(f32[2,6,256]{2,1,0:T(8,128)S(1)} %get-tuple-element.464) | copy-start | bytes 36868
  9.8 68.0 %collective-permute-start = (bf16[1,262,256]{2,1,0:T(8,128)(2,1)}, bf16[1,262,256]{2,1,0:T(8,128)(2,1)}, u32[]{:S(2)}, u32[]{:S(2)}) collective-permute-start(bf16[1,262,256]{2,1,0:T(8,128)(2,1)} %get-tuple-element.370), channel_id=1, source_target_pairs={{0,4},{4,8},{8,12},{12,0},{1,5},{5,9},{9,13},{13,1},{2,6},{6,10},{... | collective-permute-start | bytes 402440 | tf_op jit(solution)/shard_map/ppermute | solution.py:18
  12.8 65.7 %collective-permute-start.1 = (bf16[1,262,256]{2,1,0:T(8,128)(2,1)}, bf16[1,262,256]{2,1,0:T(8,128)(2,1)}, u32[]{:S(2)}, u32[]{:S(2)}) collective-permute-start(bf16[1,262,256]{2,1,0:T(8,128)(2,1)} %get-tuple-element.371), channel_id=1, source_target_pairs={{4,0},{8,4},{12,8},{0,12},{5,1},{9,5},{13,9},{1,13},{6,2},{10,6},{... | collective-permute-start | bytes 402440 | tf_op jit(solution)/shard_map/ppermute | solution.py:20
  22.0 8.0 %copy-start.48 = (f32[1,1,256]{2,1,0:T(1,128)}, f32[1,1,256]{2,1,0:T(1,128)S(1)}, u32[]{:S(2)}) copy-start(f32[1,1,256]{2,1,0:T(1,128)S(1)} %get-tuple-element.420) | copy-start | bytes 3076
  22.1 8.0 %copy-start.51 = (f32[1,1,256]{2,1,0:T(1,128)}, f32[1,1,256]{2,1,0:T(1,128)S(1)}, u32[]{:S(2)}) copy-start(f32[1,1,256]{2,1,0:T(1,128)S(1)} %get-tuple-element.421) | copy-start | bytes 3076
  22.1 8.0 %copy-start.54 = (f32[1,1,256]{2,1,0:T(1,128)}, f32[1,1,256]{2,1,0:T(1,128)S(1)}, u32[]{:S(2)}) copy-start(f32[1,1,256]{2,1,0:T(1,128)S(1)} %get-tuple-element.422) | copy-start | bytes 3076
  22.1 8.0 %copy-start.73 = (f32[1,1,256]{2,1,0:T(1,128)}, f32[1,1,256]{2,1,0:T(1,128)S(1)}, u32[]{:S(2)}) copy-start(f32[1,1,256]{2,1,0:T(1,128)S(1)} %get-tuple-element.419) | copy-start | bytes 3076
  22.1 25.9 %copy-start.57 = (f32[1,1,256]{2,1,0:T(1,128)}, f32[1,1,256]{2,1,0:T(1,128)S(1)}, u32[]{:S(2)}) copy-start(f32[1,1,256]{2,1,0:T(1,128)S(1)} %get-tuple-element.416) | copy-start | bytes 3076
  22.1 25.9 %copy-start.60 = (f32[1,1,256]{2,1,0:T(1,128)}, f32[1,1,256]{2,1,0:T(1,128)S(1)}, u32[]{:S(2)}) copy-start(f32[1,1,256]{2,1,0:T(1,128)S(1)} %get-tuple-element.426) | copy-start | bytes 3076
  22.1 25.9 %copy-start.63 = (f32[1,1,256]{2,1,0:T(1,128)}, f32[1,1,256]{2,1,0:T(1,128)S(1)}, u32[]{:S(2)}) copy-start(f32[1,1,256]{2,1,0:T(1,128)S(1)} %get-tuple-element.427) | copy-start | bytes 3076
  22.1 25.9 %copy-start.76 = (f32[1,1,256]{2,1,0:T(1,128)}, f32[1,1,256]{2,1,0:T(1,128)S(1)}, u32[]{:S(2)}) copy-start(f32[1,1,256]{2,1,0:T(1,128)S(1)} %get-tuple-element.425) | copy-start | bytes 3076
  22.1 4.1 %copy-start.154 = (f32[256]{0:T(256)}, f32[256]{0:T(256)S(1)}, u32[]{:S(2)}) copy-start(f32[256]{0:T(256)S(1)} %get-tuple-element.524) | copy-start | bytes 3076
  22.1 7.9 %copy-start.152 = (f32[256]{0:T(256)}, f32[256]{0:T(256)S(1)}, u32[]{:S(2)}) copy-start(f32[256]{0:T(256)S(1)} %get-tuple-element.523) | copy-start | bytes 3076
  22.8 7.8 %copy-start.34 = (f32[1,1,256]{2,1,0:T(1,128)}, f32[1,1,256]{2,1,0:T(1,128)S(1)}, u32[]{:S(2)}) copy-start(f32[1,1,256]{2,1,0:T(1,128)S(1)} %get-tuple-element.395) | copy-start | bytes 3076
  22.8 7.8 %copy-start.36 = (f32[1,1,256]{2,1,0:T(1,128)}, f32[1,1,256]{2,1,0:T(1,128)S(1)}, u32[]{:S(2)}) copy-start(f32[1,1,256]{2,1,0:T(1,128)S(1)} %get-tuple-element.397) | copy-start | bytes 3076
  22.8 7.8 %copy-start.66 = (f32[1,1,256]{2,1,0:T(1,128)}, f32[1,1,256]{2,1,0:T(1,128)S(1)}, u32[]{:S(2)}) copy-start(f32[1,1,256]{2,1,0:T(1,128)S(1)} %get-tuple-element.394) | copy-start | bytes 3076
  22.8 22.0 %copy-start.31 = (f32[1,1,256]{2,1,0:T(1,128)}, f32[1,1,256]{2,1,0:T(1,128)S(1)}, u32[]{:S(2)}) copy-start(f32[1,1,256]{2,1,0:T(1,128)S(1)} %get-tuple-element.406) | copy-start | bytes 3076
  22.8 22.0 %copy-start.42 = (f32[1,1,256]{2,1,0:T(1,128)}, f32[1,1,256]{2,1,0:T(1,128)S(1)}, u32[]{:S(2)}) copy-start(f32[1,1,256]{2,1,0:T(1,128)S(1)} %get-tuple-element.405) | copy-start | bytes 3076
  22.8 22.0 %copy-start.45 = (f32[1,1,256]{2,1,0:T(1,128)}, f32[1,1,256]{2,1,0:T(1,128)S(1)}, u32[]{:S(2)}) copy-start(f32[1,1,256]{2,1,0:T(1,128)S(1)} %get-tuple-element.392) | copy-start | bytes 3076
  22.8 22.0 %copy-start.70 = (f32[1,1,256]{2,1,0:T(1,128)}, f32[1,1,256]{2,1,0:T(1,128)S(1)}, u32[]{:S(2)}) copy-start(f32[1,1,256]{2,1,0:T(1,128)S(1)} %get-tuple-element.404) | copy-start | bytes 3076
  22.8 25.2 %copy-start.38 = (f32[1,1,256]{2,1,0:T(1,128)}, f32[1,1,256]{2,1,0:T(1,128)S(1)}, u32[]{:S(2)}) copy-start(f32[1,1,256]{2,1,0:T(1,128)S(1)} %get-tuple-element.400) | copy-start | bytes 3076
  22.8 25.2 %copy-start.40 = (f32[1,1,256]{2,1,0:T(1,128)}, f32[1,1,256]{2,1,0:T(1,128)S(1)}, u32[]{:S(2)}) copy-start(f32[1,1,256]{2,1,0:T(1,128)S(1)} %get-tuple-element.402) | copy-start | bytes 3076
  22.9 25.2 %copy-start.68 = (f32[1,1,256]{2,1,0:T(1,128)}, f32[1,1,256]{2,1,0:T(1,128)S(1)}, u32[]{:S(2)}) copy-start(f32[1,1,256]{2,1,0:T(1,128)S(1)} %get-tuple-element.399) | copy-start | bytes 3076
  22.9 5.9 %copy-start.128 = (f32[256]{0:T(256)}, f32[256]{0:T(256)S(1)}, u32[]{:S(2)}) copy-start(f32[256]{0:T(256)S(1)} %get-tuple-element.543) | copy-start | bytes 3076
  22.9 23.0 %copy-start.126 = (f32[256]{0:T(256)}, f32[256]{0:T(256)S(1)}, u32[]{:S(2)}) copy-start(f32[256]{0:T(256)S(1)} %get-tuple-element.542) | copy-start | bytes 3076
  22.9 7.1 %copy-start.124 = (f32[256]{0:T(256)}, f32[256]{0:T(256)S(1)}, u32[]{:S(2)}) copy-start(f32[256]{0:T(256)S(1)} %integer_pow.265) | copy-start | bytes 3076
  23.5 20.3 %copy-start.134 = (f32[256]{0:T(256)}, f32[256]{0:T(256)S(1)}, u32[]{:S(2)}) copy-start(f32[256]{0:T(256)S(1)} %get-tuple-element.533) | copy-start | bytes 3076
  23.5 31.0 %copy-start.132 = (f32[256]{0:T(256)}, f32[256]{0:T(256)S(1)}, u32[]{:S(2)}) copy-start(f32[256]{0:T(256)S(1)} %get-tuple-element.532) | copy-start | bytes 3076
  23.5 22.7 %copy-start.130 = (f32[256]{0:T(256)}, f32[256]{0:T(256)S(1)}, u32[]{:S(2)}) copy-start(f32[256]{0:T(256)S(1)} %integer_pow.259) | copy-start | bytes 3076
  23.6 28.6 %copy-start.136 = (f32[256]{0:T(256)}, f32[256]{0:T(256)S(1)}, u32[]{:S(2)}) copy-start(f32[256]{0:T(256)S(1)} %integer_pow.253) | copy-start | bytes 3076
  24.1 5.9 %copy-start.90 = (f32[128]{0:T(128)}, f32[128]{0:T(128)S(1)}, u32[]{:S(2)}) copy-start(f32[128]{0:T(128)S(1)} %get-tuple-element.474) | copy-start | bytes 1540
  24.1 23.9 %copy-start.93 = (f32[128]{0:T(128)}, f32[128]{0:T(128)S(1)}, u32[]{:S(2)}) copy-start(f32[128]{0:T(128)S(1)} %get-tuple-element.294) | copy-start | bytes 1540
  24.7 2.1 copy-start.140
  24.7 3.5 %copy-start.142 = (f32[256]{0:T(256)}, f32[256]{0:T(256)S(1)}, u32[]{:S(2)}) copy-start(f32[256]{0:T(256)S(1)} %get-tuple-element.628) | copy-start | bytes 3076
  24.8 3.8 %copy-start.138 = (f32[256]{0:T(256)}, f32[256]{0:T(256)S(1)}, u32[]{:S(2)}) copy-start(f32[256]{0:T(256)S(1)} %get-tuple-element.546) | copy-start | bytes 3076
  24.8 5.8 %copy-start.144 = (f32[256]{0:T(256)}, f32[256]{0:T(256)S(1)}, u32[]{:S(2)}) copy-start(f32[256]{0:T(256)S(1)} %get-tuple-element.629) | copy-start | bytes 3076
  26.0 18.9 %copy-start.146 = (f32[256]{0:T(256)}, f32[256]{0:T(256)S(1)}, u32[]{:S(2)}) copy-start(f32[256]{0:T(256)S(1)} %get-tuple-element.622) | copy-start | bytes 3076
  26.0 18.9 %copy-start.150 = (f32[256]{0:T(256)}, f32[256]{0:T(256)S(1)}, u32[]{:S(2)}) copy-start(f32[256]{0:T(256)S(1)} %get-tuple-element.536) | copy-start | bytes 3076
  26.0 22.1 %copy-start.148 = (f32[256]{0:T(256)}, f32[256]{0:T(256)S(1)}, u32[]{:S(2)}) copy-start(f32[256]{0:T(256)S(1)} %get-tuple-element.623) | copy-start | bytes 3076
  26.0 4.6 %copy-start.80 = (f32[128]{0:T(128)}, f32[128]{0:T(128)S(1)}, u32[]{:S(2)}) copy-start(f32[128]{0:T(128)S(1)} %get-tuple-element.478) | copy-start | bytes 1540
  26.0 18.9 %copy-start.86 = (f32[128]{0:T(128)}, f32[128]{0:T(128)S(1)}, u32[]{:S(2)}) copy-start(f32[128]{0:T(128)S(1)} %get-tuple-element.476) | copy-start | bytes 1540
  26.0 22.0 %copy-start.83 = (f32[128]{0:T(128)}, f32[128]{0:T(128)S(1)}, u32[]{:S(2)}) copy-start(f32[128]{0:T(128)S(1)} %get-tuple-element.477) | copy-start | bytes 1540
  41.4 16.0 %copy-start.7 = (bf16[4,256,256]{2,1,0:T(8,128)(2,1)}, bf16[4,256,256]{2,1,0:T(8,128)(2,1)S(1)}, u32[]{:S(2)}) copy-start(bf16[4,256,256]{2,1,0:T(8,128)(2,1)S(1)} %all_gather.7) | copy-start | bytes 1572868
  65.8 7.2 %copy-start.2 = (f32[896,256]{1,0:T(8,128)}, f32[896,256]{1,0:T(8,128)S(1)}, u32[]{:S(2)}) copy-start(f32[896,256]{1,0:T(8,128)S(1)} %fusion.152) | copy-start | bytes 2752516
  67.9 1.5 copy-start
  67.9 1.5 copy-start.118
  86.3 7.5 %copy-start.201 = (f32[128]{0:T(128)}, f32[128]{0:T(128)S(1)}, u32[]{:S(2)}) copy-start(f32[128]{0:T(128)S(1)} %get-tuple-element.630) | copy-start | bytes 1540
  89.2 41.4 %collective-permute-start.3 = (bf16[1,262,256]{2,1,0:T(8,128)(2,1)}, bf16[1,262,256]{2,1,0:T(8,128)(2,1)}, u32[]{:S(2)}, u32[]{:S(2)}) collective-permute-start(bf16[1,262,256]{2,1,0:T(8,128)(2,1)} %maximum_bitcast_fusion.1), channel_id=1, source_target_pairs={{4,0},{8,4},{12,8},{0,12},{5,1},{9,5},{13,9},{1,13},{6,2},{10,6},{... | collective-permute-start | bytes 402440 | tf_op jit(solution)/shard_map/ppermute | solution.py:20
  91.3 3.9 %copy-start.3 = (f32[896,256]{1,0:T(8,128)S(1)}, f32[896,256]{1,0:T(8,128)}, u32[]{:S(2)}) copy-start(f32[896,256]{1,0:T(8,128)} %copy-done.2) | copy-start | bytes 2752516
  92.9 2.2 copy-start.123
  93.6 37.1 %collective-permute-start.2 = (bf16[1,262,256]{2,1,0:T(8,128)(2,1)}, bf16[1,262,256]{2,1,0:T(8,128)(2,1)}, u32[]{:S(2)}, u32[]{:S(2)}) collective-permute-start(bf16[1,262,256]{2,1,0:T(8,128)(2,1)} %maximum_bitcast_fusion), channel_id=1, source_target_pairs={{0,4},{4,8},{8,12},{12,0},{1,5},{5,9},{9,13},{13,1},{2,6},{6,10},{... | collective-permute-start | bytes 402440 | tf_op jit(solution)/shard_map/ppermute | solution.py:18
  97.6 1.6 copy-start.1
  97.6 1.6 copy-start.119
  101.3 2.7 %copy-start.115 = (f32[1,1,256]{2,1,0:T(1,128)S(1)}, f32[1,1,256]{2,1,0:T(1,128)}, u32[]{:S(2)}) copy-start(f32[1,1,256]{2,1,0:T(1,128)} %get-tuple-element.408) | copy-start | bytes 3076
  106.9 2.6 %copy-start.111 = (f32[1,1,256]{2,1,0:T(1,128)S(1)}, f32[1,1,256]{2,1,0:T(1,128)}, u32[]{:S(2)}) copy-start(f32[1,1,256]{2,1,0:T(1,128)} %get-tuple-element.407) | copy-start | bytes 3076
  115.7 55.9 %reduce-scatter.5.cloned.1.call-start = ((), (), s32[]{:S(2)}) async-start(), calls=%async_computation.5 | async-start | bytes 49152 | tf_op jit(solution)/shard_map/reduce_scatter | solution.py:352
  122.5 1.8 copy-start.170
  122.5 1.8 copy-start.171
  122.6 3.0 %copy-start.6 = (f32[896,256]{1,0:T(8,128)S(1)}, f32[896,256]{1,0:T(8,128)}, u32[]{:S(2)}) copy-start(f32[896,256]{1,0:T(8,128)} %fusion.150) | copy-start | bytes 2752516
  127.5 2.8 %copy-start.11 = (bf16[7,128,256]{1,2,0:T(8,128)(2,1)S(1)}, bf16[7,128,256]{1,2,0:T(8,128)(2,1)}, u32[]{:S(2)}) copy-start(bf16[7,128,256]{1,2,0:T(8,128)(2,1)} %copy-done.10) | copy-start | bytes 1376260
  128.8 82.6 %all-reduce.151.cloned.1.call-start = ((), (), s32[]{:S(2)}) async-start(), calls=%async_computation.2 | async-start | bytes 1048576 | tf_op jit(solution)/shard_map/psum | solution.py:349
  133.7 92.9 %all-reduce.153.cloned.1.call-start = ((), (), s32[]{:S(2)}) async-start(), calls=%async_computation.4 | async-start | bytes 1048576 | tf_op jit(solution)/shard_map/psum | solution.py:354
  226.5 1.9 copy-start.17
  (151 other events, 126.4 us)
Sparse Core Ops, SparseCore 0:
  115.8 21.4 reduce-scatter.2
  139.5 9.7 reduce-scatter.4
Sparse Core Ops, SparseCore 1:
  133.8 34.4 all-reduce.150
  170.5 56.0 all-reduce.152
where the time goes:
time: 240 us; the launch traced here: 238 us
  blocking collectives  82.1 us (34%)
  other arithmetic  54.3 us (23%)
  local copies, waits for them, and re-layouts  33.1 us (14%)
  matrix products  21.1 us (9%)
  between operations  21.1 us (9%)
  waiting for transfers between devices  18.9 us (8%)
  starting transfers between devices  7.24 us (3%)
    psum x1, blocking collectives, shards(): lax.psum((jnp.sum(residual * residual), live_count[0].astype(jnp.float32)...  32.8 us
    unnamed x420, local copies, waits for them, and re-layouts  27.4 us
    psum x1, blocking collectives, shards(): coarse_sums = lax.psum((owned[0], owned[1]), ('sub', 'rep'))  26.6 us
    unnamed x31, other arithmetic  20.1 us
    psum x1, waiting for transfers between devices, shards(): coarse_sums = lax.psum((owned[0], owned[1]), ('sub', 'rep'))  15.2 us
    psum x1, blocking collectives, shards(): fine_sums = lax.psum((fine_gh, fine_ge), ('blk', 'rep'))  10.5 us
    dot_general x7, matrix products, net_backward(): lax.dot_general(flat_streams, grad_low, (((0,), (0,)), ((), ())), preferr...  10.2 us
    all_gather x1, blocking collectives, shards(): lax.all_gather(coarse_hidden, 'blk', axis=0, tiled=True)  7.82 us
  transfers between devices with their start and end apart: 8, of which 2 were waited for; matrix products, arithmetic and copies ran while one was open for 31% of the time, Pallas kernels for 0%

commit v1 on v0

v1 whole, which is shorter than its diff:
```python
import functools

import jax
import jax.numpy as jnp
from jax import lax
from jax.experimental import pallas as pl
from jax.experimental.pallas import tpu as pltpu
from jax.sharding import PartitionSpec as P

MESH = pl.DeviceIdType.MESH
F32 = jnp.float32
BF16 = jnp.bfloat16
WIDTH_SQ = 0.36
CHUNK = 16
UNROLL = 2
EXACT = lax.Precision.HIGHEST


def wide(tile, columns):
    return jnp.concatenate([tile] * (columns // tile.shape[1]), axis=1)


def fold(value):
    total = value[0:8]
    for at in range(8, value.shape[0], 8):
        total = total + value[at : at + 8]
    return total


def rows_of(step):
    return pl.ds(pl.multiple_of(step * CHUNK, CHUNK), CHUNK)


def window_rows(dx, width_sq, speed):
    weight = jnp.exp(-dx * dx / width_sq)
    weight_x = -2.0 * dx / width_sq * weight
    weight_xx = (4.0 * dx * dx / (width_sq * width_sq) - 2.0 / width_sq) * weight
    return (weight, speed * weight, 2.0 * speed * weight_x, speed * weight_xx)


class Net:
    def __init__(self, count, factors, edge, weights, cols, offset, ids, streams, layers, hidden):
        self.count, self.factors = count, factors
        self.edge, self.weights = edge, weights
        self.cols, self.offset, self.ids = cols, offset, ids
        self.streams, self.layers, self.hidden = streams, layers, hidden

    def col(self, name, step):
        at = self.ids[name]
        rows = pl.ds(pl.multiple_of(self.offset + step * CHUNK, CHUNK), CHUNK)
        return self.cols[rows, at : at + 1]

    def forward(self, totals):
        edge = self.edge()
        e = [edge[j : j + 1] for j in range(6)]
        columns = edge.shape[1]
        scaled = [self.factors[d] * e[d] for d in range(3)]
        squares = [s * s for s in scaled]

        def first(step, carry):
            rows = rows_of(step)
            pre = (
                self.col("t", step) * e[0]
                + self.col("x", step) * e[1]
                + self.col("y", step) * e[2]
                + e[3]
            )
            h = jnp.tanh(pre)
            g = 1.0 - h * h
            s = -2.0 * h * g
            self.hidden[rows, :] = h
            self.streams[0, rows, :] = h.astype(BF16)
            for d in range(3):
                self.streams[1 + d, rows, :] = (g * scaled[d]).astype(BF16)
                self.streams[4 + d, rows, :] = (s * squares[d]).astype(BF16)
            return carry

        steps = self.count // CHUNK
        lax.fori_loop(0, steps, first, 0, unroll=UNROLL)
        flat = self.streams[...].reshape(7 * self.count, columns)
        self.layers[...] = jnp.dot(
            flat, self.weights(), preferred_element_type=F32
        ).reshape(7, self.count, columns)
        out = e[5] * (1.0 / float(columns) ** 0.5)

        def second(step, carry):
            rows = rows_of(step)
            w, cw = self.col("w", step), self.col("cw", step)
            cx, cxx = self.col("cx", step), self.col("cxx", step)
            k = jnp.tanh(self.layers[0, rows, :] + e[4])
            m = 1.0 - k * k
            l1, l2, l3 = [self.layers[j, rows, :] for j in (1, 2, 3)]
            curved = (
                w * self.layers[4, rows, :]
                - cw * (self.layers[5, rows, :] + self.layers[6, rows, :])
                - cx * l2
            )
            q = w * (l1 * l1) - cw * (l2 * l2 + l3 * l3)
            v = curved - 2.0 * k * q
            t = m * v - cxx * k
            self.layers[0, rows, :] = k
            self.layers[4, rows, :] = v
            self.layers[5, rows, :] = q
            self.layers[6, rows, :] = t
            value = jnp.sum(t * out, axis=1, keepdims=True)
            at = pl.ds(pl.multiple_of(self.offset + step * CHUNK, CHUNK), CHUNK)
            totals[at, :] = totals[at, :] + jnp.broadcast_to(value, (CHUNK, 128))
            return carry

        lax.fori_loop(0, steps, second, 0, unroll=UNROLL)

    def backward(self, cotangent, grads, grad_out, edge_out):
        edge = self.edge()
        e = [edge[j : j + 1] for j in range(6)]
        columns = edge.shape[1]
        norm = 1.0 / float(columns) ** 0.5
        out = e[5] * norm
        scaled = [self.factors[d] * e[d] for d in range(3)]
        squares = [s * s for s in scaled]
        zero = jnp.zeros((8, columns), F32)
        steps = self.count // CHUNK
        low = grads.at[:, pl.ds(0, self.count), :]

        def first(step, carry):
            rows = rows_of(step)
            at = pl.ds(pl.multiple_of(self.offset + step * CHUNK, CHUNK), CHUNK)
            cot = wide(cotangent[at, :], columns)
            w, cw = self.col("w", step), self.col("cw", step)
            cx, cxx = self.col("cx", step), self.col("cxx", step)
            k, l1, l2, l3, v, q, t = [self.layers[j, rows, :] for j in range(7)]
            m = 1.0 - k * k
            com = cot * out * m
            k4 = 4.0 * k * com
            kc = k4 * cw
            g0 = com * (-2.0 * (k * v + m * q) - cxx)
            low[0, rows, :] = g0.astype(BF16)
            low[1, rows, :] = (-(k4 * w) * l1).astype(BF16)
            low[2, rows, :] = (kc * l2 - com * cx).astype(BF16)
            low[3, rows, :] = (kc * l3).astype(BF16)
            low[4, rows, :] = (com * w).astype(BF16)
            minus = (-(com * cw)).astype(BF16)
            low[5, rows, :] = minus
            low[6, rows, :] = minus
            return (carry[0] + fold(g0), carry[1] + fold(cot * t))

        sum4, sum5 = lax.fori_loop(0, steps, first, (zero, zero), unroll=UNROLL)
        flat = self.streams[...].reshape(7 * self.count, columns)
        flat_low = low[...].reshape(7 * self.count, columns)
        grad_out(
            lax.dot_general(
                flat, flat_low, (((0,), (0,)), ((), ())), preferred_element_type=F32
            )
        )
        self.layers[...] = lax.dot_general(
            flat_low, self.weights(), (((1,), (1,)), ((), ())), preferred_element_type=F32
        ).reshape(7, self.count, columns)

        def second(step, carry):
            rows = rows_of(step)
            h = self.hidden[rows, :]
            i = [self.layers[j, rows, :] for j in range(7)]
            h2 = h * h
            g = 1.0 - h2
            s = -2.0 * h * g
            lin = i[1] * scaled[0] + i[2] * scaled[1] + i[3] * scaled[2]
            quad = i[4] * squares[0] + i[5] * squares[1] + i[6] * squares[2]
            da = g * (i[0] - 2.0 * h * lin + (6.0 * h2 - 2.0) * quad)
            terms = [
                da,
                da * self.col("t", step),
                da * self.col("x", step),
                da * self.col("y", step),
            ]
            terms += [g * i[1 + d] for d in range(3)] + [s * i[4 + d] for d in range(3)]
            return tuple(c + fold(x) for c, x in zip(carry, terms))

        sums = lax.fori_loop(0, steps, second, (zero,) * 10, unroll=UNROLL)
        sums = [jnp.sum(x, axis=0, keepdims=True) for x in sums]
        rows = [
            sums[1 + d]
            + self.factors[d] * sums[4 + d]
            + 2.0 * self.factors[d] * scaled[d] * sums[7 + d]
            for d in range(3)
        ]
        rows.append(sums[0])
        rows.append(jnp.sum(sum4, axis=0, keepdims=True))
        rows.append(jnp.sum(sum5, axis=0, keepdims=True) * norm)
        for j, row in enumerate(rows):
            edge_out(j, row)


def kernel(
    S, B, CB, FD, points_ref, source_ref, speed_ref, live_ref, index_ref, fh_ref, fe_ref, ch_ref,
    ce_ref, res_out, fgh_out, fge_out, cgh_out, cge_out, loss_out,
    call, cedge, fedge, wl, wr, edge_l, edge_r, rows_sc, cols, lrows, lcols, pick_t, pick,
    totals, ltotals, cot, lcot, idx_sc, st, layers, hid, stl, ll, hl, grads,
    gh, gr, cge, cge_r, lge, lge_r, fge, fge_r,
    cown, cst, cxr, csum, zst, zr, zg, zg2, cex, cez, fown, fst, fxr, nst, nz, lex, lez, fex,
    fag, fg, fg2,
    w_send, w_recv, chip_send, chip_recv, x_send, x_recv, z_send, z_recv, a_send, a_recv,
):
    C = CB * B
    PS = S // CB
    NP = points_ref.shape[1]
    cap = index_ref.shape[1]
    H = fh_ref.shape[1]
    s, b, r = lax.axis_index("sub"), lax.axis_index("blk"), lax.axis_index("rep")
    other = 1 - r
    right, left = lax.rem(s + 1, S), lax.rem(s + S - 1, S)
    cell = s // max(S // C, 1)
    half_width = float(FD * S) / float(C)

    barrier = pltpu.get_barrier_semaphore()
    pl.semaphore_signal(barrier, inc=1, device_id={"rep": other}, device_id_type=MESH)
    for d in range(1, B):
        pl.semaphore_signal(
            barrier, inc=1, device_id={"blk": lax.rem(b + d, B)}, device_id_type=MESH
        )
    for d in range(1, S):
        pl.semaphore_signal(
            barrier, inc=1, device_id={"sub": lax.rem(s + d, S)}, device_id_type=MESH
        )

    fedge[...] = jnp.zeros_like(fedge)
    for k in range(FD):
        fedge[k, 0:6, :] = fe_ref[k].astype(F32)
    for k in range(CB):
        cedge[b * CB + k] = jnp.concatenate(
            [ce_ref[k].astype(F32), jnp.zeros((2, H), F32)], axis=0
        )
        call[b * CB + k] = ch_ref[k]
    pl.semaphore_wait(barrier, S + B - 1)

    def remote(src, dst, send, recv, **where):
        copy = pltpu.make_async_remote_copy(
            src_ref=src, dst_ref=dst, send_sem=send, recv_sem=recv,
            device_id=where, device_id_type=MESH,
        )
        copy.start()
        return copy

    wcopies = [
        remote(fh_ref.at[0], wr, w_send.at[0], w_recv.at[0], sub=left),
        remote(fh_ref.at[FD - 1], wl, w_send.at[1], w_recv.at[1], sub=right),
        remote(fedge.at[0], edge_r, w_send.at[2], w_recv.at[2], sub=left),
        remote(fedge.at[FD - 1], edge_l, w_send.at[3], w_recv.at[3], sub=right),
    ]
    mine = pl.ds(b * CB, CB)
    xcopies = []
    for d in range(1, B):
        to = lax.rem(b + d, B)
        xcopies.append(
            remote(ch_ref, call.at[mine], w_send.at[2 + 2 * d], w_recv.at[2 + 2 * d], blk=to)
        )
        xcopies.append(
            remote(
                cedge.at[mine], cedge.at[mine], w_send.at[3 + 2 * d], w_recv.at[3 + 2 * d], blk=to
            )
        )

    start = s.astype(F32) * FD
    t_row, x_row, y_row = points_ref[0:1, :], points_ref[1:2, :], points_ref[2:3, :]
    speed_row = speed_ref[...]
    rows_sc[...] = jnp.zeros_like(rows_sc)
    rows_sc[0:1, :] = 2.0 * (t_row - 0.5)
    rows_sc[1:2, :] = 2.0 * (y_row - 0.5)
    rows_sc[2:3, :] = source_ref[...]
    ids = []
    for e in range(FD + 3):
        if e < FD:
            dx = x_row - (start + (e + 0.5))
            width, z = WIDTH_SQ, 2.0 * dx
        else:
            dx = x_row - (cell.astype(F32) + (e - FD - 0.5)) * half_width
            width, z = WIDTH_SQ * half_width * half_width, 2.0 * dx / half_width
        at = 3 + 5 * e
        rows_sc[at : at + 1, :] = z
        for j, row in enumerate(window_rows(dx, width, speed_row)):
            rows_sc[at + 1 + j : at + 2 + j, :] = row
        ids.append({"t": 0, "y": 1, "x": at, "w": at + 1, "cw": at + 2, "cx": at + 3, "cxx": at + 4})
    cols[...] = rows_sc[...].T
    idx_sc[...] = jnp.full_like(idx_sc, -1)
    idx_sc[0:1, 0:cap] = index_ref[0:1, :]
    idx_sc[0:1, cap : 2 * cap] = index_ref[1:2, :]
    pick_t[...] = (
        lax.broadcasted_iota(jnp.int32, (NP, 128), 0) == idx_sc[0:1, :]
    ).astype(F32)
    pick[...] = pick_t[...].T
    fields = jnp.concatenate(
        [points_ref[...], speed_row, jnp.zeros((4, NP), F32)], axis=0
    )
    listed = jnp.dot(fields, pick_t[...], preferred_element_type=F32, precision=EXACT)
    is_left = lax.broadcasted_iota(jnp.int32, (1, 128), 1) < cap
    dx = listed[1:2] - jnp.where(is_left, start - 0.5, start + (FD + 0.5))
    lrows[...] = jnp.zeros_like(lrows)
    lrows[0:1, :] = 2.0 * (listed[0:1] - 0.5)
    lrows[1:2, :] = 2.0 * (listed[2:3] - 0.5)
    lrows[3:4, :] = 2.0 * dx
    for j, row in enumerate(window_rows(dx, WIDTH_SQ, listed[3:4])):
        lrows[4 + j : 5 + j, :] = row
    lcols[...] = lrows[...].T
    lids = ids[0]

    fine_f = (2.0, 2.0, 2.0)
    coarse_f = (2.0, 2.0 / half_width, 2.0)
    fine = [
        Net(NP, fine_f, lambda k=k: fedge[k], lambda k=k: fh_ref[k], cols, 0, ids[k],
            st.at[k], layers.at[k], hid.at[k])
        for k in range(FD)
    ]
    cids = [lax.rem(cell + (u + C - 1), C) for u in range(3)]
    coarse = [
        Net(NP, coarse_f, lambda u=u: cedge[cids[u]], lambda u=u: call[cids[u]], cols, 0,
            ids[FD + u], st.at[FD + u], layers.at[FD + u], hid.at[FD + u])
        for u in range(3)
    ]
    lists = [
        Net(cap, fine_f, lambda: edge_l[...], lambda: wl[...], lcols, 0, lids,
            stl.at[0], ll.at[0], hl.at[0]),
        Net(cap, fine_f, lambda: edge_r[...], lambda: wr[...], lcols, cap, lids,
            stl.at[1], ll.at[1], hl.at[1]),
    ]

    totals[...] = jnp.zeros_like(totals)
    ltotals[...] = jnp.zeros_like(ltotals)
    for net in fine:
        net.forward(totals)
    for copy in xcopies:
        copy.wait()
    for net in coarse:
        net.forward(totals)
    for copy in wcopies:
        copy.wait()
    for net in lists:
        net.forward(ltotals)

    total = totals[...] + jnp.dot(
        pick_t[...], ltotals[...], preferred_element_type=F32, precision=EXACT
    )
    count = live_ref[0]
    live = (lax.broadcasted_iota(jnp.int32, (NP, 128), 0) < count).astype(F32)
    residual = (total * 0.125 - cols[:, 2:3]) * live
    res_out[...] = residual.T[0:1, :]
    cot[...] = residual * 0.125
    lcot[...] = jnp.dot(pick[...], cot[...], preferred_element_type=F32, precision=EXACT)
    loss_row = wide(jnp.sum(residual * residual, axis=0, keepdims=True), H)
    count_row = jnp.full((1, H), 1.0, F32) * count.astype(F32)
    blank = jnp.concatenate([jnp.zeros((6, H), F32), loss_row, count_row], axis=0)
    for c in range(C):
        cge[c] = blank
    lge[...] = jnp.zeros_like(lge)
    fge[...] = jnp.zeros_like(fge)
    cown[...] = jnp.zeros_like(cown)
    cst[...] = jnp.zeros_like(cst)

    def run_back(e, net, cotangent, edge_ref, edge_at):
        def keep(value):
            gh[e] = value.reshape(gh.shape[1:])

        def keep_edge(j, row):
            edge_ref[edge_at, j : j + 1, :] = row

        net.backward(cotangent, grads, keep, keep_edge)
        return remote(
            gh.at[e, other], gr.at[e], chip_send.at[e], chip_recv.at[e], rep=other
        )

    NE = FD + 5
    chip = {}
    for u in range(3):
        chip[u] = run_back(u, coarse[u], cot, cge, cids[u])
    chip["ce"] = remote(cge, cge_r, chip_send.at[NE], chip_recv.at[NE], rep=other)
    for n in range(2):
        chip[3 + n] = run_back(3 + n, lists[n], lcot, lge, n)
    chip["le"] = remote(lge, lge_r, chip_send.at[NE + 1], chip_recv.at[NE + 1], rep=other)

    for u in range(3):
        chip[u].wait()
        value = (gh[u, r] + gr[u]).reshape(cown.shape[1:])
        cown[cids[u]] = value
        cst[cids[u]] = value.astype(cst.dtype)
    chip["ce"].wait()
    cge[...] = cge[...] + cge_r[...]
    cex[b] = cge[mine]
    cx = []
    for d in range(1, B):
        to = lax.rem(b + d, B)
        theirs = pl.ds(to * CB, CB)
        cx.append(
            remote(cst.at[theirs], cxr.at[b], x_send.at[d, 0], x_recv.at[d, 0], blk=to)
        )
        cx.append(
            remote(cge.at[theirs], cex.at[b], x_send.at[d, 1], x_recv.at[d, 1], blk=to)
        )

    chip[5] = run_back(5, fine[0], cot, fge, 0)

    def share(e, n):
        chip[e].wait()
        fown[n] = gh[e, r, b] + gr[e, b]
        for d in range(1, B):
            to = lax.rem(b + d, B)
            fst[to, n] = (gh[e, r, to] + gr[e, to]).astype(BF16)

    for n in range(2):
        share(3 + n, n)
    chip["le"].wait()
    lge[...] = lge[...] + lge_r[...]
    lex[b] = lge[...]
    lx = []
    for d in range(1, B):
        to = lax.rem(b + d, B)
        lx.append(
            remote(fst.at[to, pl.ds(0, 2)], fxr.at[b, pl.ds(0, 2)], x_send.at[d, 2],
                   x_recv.at[d, 2], blk=to)
        )
        lx.append(remote(lge, lex.at[b], x_send.at[d, 3], x_recv.at[d, 3], blk=to))

    for copy in cx:
        copy.wait()
    for k in range(CB):
        value = cown[b * CB + k]
        for d in range(1, B):
            value = value + cxr[lax.rem(b + d, B), k].astype(F32)
        csum[k] = value
        zst[k] = value.astype(zst.dtype)
    edge_sum = cex[0]
    for d in range(1, B):
        edge_sum = edge_sum + cex[d]
    cez[s] = edge_sum
    cz = []
    for d in range(1, S):
        to = lax.rem(s + d, S)
        cz.append(
            remote(zst.at[to // PS, lax.rem(to, PS)], zr.at[s], z_send.at[d, 0],
                   z_recv.at[d, 0], sub=to)
        )
        cz.append(remote(cez.at[s], cez.at[s], z_send.at[d, 1], z_recv.at[d, 1], sub=to))

    for k in range(1, FD):
        chip[5 + k] = run_back(5 + k, fine[k], cot, fge, k)
    chip["fe"] = remote(fge, fge_r, chip_send.at[NE + 2], chip_recv.at[NE + 2], rep=other)

    for copy in lx:
        copy.wait()
    for n in range(2):
        value = fown[n]
        for d in range(1, B):
            value = value + fxr[lax.rem(b + d, B), n].astype(F32)
        nst[n] = value.astype(BF16)
    edge_sum = lex[0]
    for d in range(1, B):
        edge_sum = edge_sum + lex[d]
    lge[...] = edge_sum
    nx = [
        remote(nst.at[0], nz.at[1], a_send.at[0], a_recv.at[0], sub=left),
        remote(nst.at[1], nz.at[0], a_send.at[1], a_recv.at[1], sub=right),
        remote(lge.at[0], lez.at[1], a_send.at[2], a_recv.at[2], sub=left),
        remote(lge.at[1], lez.at[0], a_send.at[3], a_recv.at[3], sub=right),
    ]

    for k in range(FD):
        share(5 + k, 2 + k)
    chip["fe"].wait()
    fge[...] = fge[...] + fge_r[...]
    fex[b] = fge[...]
    fx = []
    for d in range(1, B):
        to = lax.rem(b + d, B)
        fx.append(
            remote(fst.at[to, pl.ds(2, FD)], fxr.at[b, pl.ds(2, FD)], x_send.at[d, 4],
                   x_recv.at[d, 4], blk=to)
        )
        fx.append(remote(fge, fex.at[b], x_send.at[d, 5], x_recv.at[d, 5], blk=to))

    for copy in cz:
        copy.wait()
    piece = csum[s // PS, lax.rem(s, PS)]
    for d in range(1, S):
        piece = piece + zr[lax.rem(s + d, S)].astype(F32)
    zg[s] = piece.astype(zg.dtype)
    cg = []
    for d in range(1, S):
        to = lax.rem(s + d, S)
        cg.append(remote(zg.at[s], zg.at[s], z_send.at[d, 2], z_recv.at[d, 2], sub=to))
    cf = [remote(zg.at[s], zg2.at[s], z_send.at[0, 0], z_recv.at[0, 0], rep=other)]
    edge_sum = cez[0]
    for d in range(1, S):
        edge_sum = edge_sum + cez[d]
    for k in range(CB):
        cge_out[k] = edge_sum[k, 0:6, :]
    loss_out[...] = edge_sum[0, 6:7, 0:128] / edge_sum[0, 7:8, 0:128]

    for copy in fx + nx:
        copy.wait()
    for k in range(FD):
        value = fown[2 + k]
        for d in range(1, B):
            value = value + fxr[lax.rem(b + d, B), 2 + k].astype(F32)
        if k == 0:
            value = value + nz[0].astype(F32)
        if k == FD - 1:
            value = value + nz[1].astype(F32)
        fg[b, k] = value.astype(BF16)
    fgc = []
    for d in range(1, B):
        to = lax.rem(b + d, B)
        fgc.append(remote(fg.at[b], fg.at[b], a_send.at[4 + d], a_recv.at[4 + d], blk=to))
    ff = [remote(fg.at[b], fg2.at[b], a_send.at[4], a_recv.at[4], rep=other)]
    edge_sum = fex[0]
    for d in range(1, B):
        edge_sum = edge_sum + fex[d]
    for k in range(FD):
        value = edge_sum[k]
        if k == 0:
            value = value + lez[0]
        if k == FD - 1:
            value = value + lez[1]
        fge_out[k] = value[0:6, :]

    for d in range(1, B):
        fgc[d - 1].wait()
        src = lax.rem(b + B - d, B)
        ff.append(
            remote(fg.at[src], fg2.at[src], a_send.at[4 + B - 1 + d], a_recv.at[4 + B - 1 + d],
                   rep=other)
        )
    for d in range(1, S):
        cg[d - 1].wait()
        src = lax.rem(s + S - d, S)
        cf.append(
            remote(zg.at[src], zg2.at[src], z_send.at[d, 3], z_recv.at[d, 3], rep=other)
        )
    for q in range(B):
        for k in range(FD):
            fgh_out[k, r, q] = fg[q, k].astype(F32)
    for p in range(S):
        cgh_out[p // PS, r, p % PS] = zg[p].astype(F32)
    for copy in ff:
        copy.wait()
    for q in range(B):
        for k in range(FD):
            fgh_out[k, other, q] = fg2[q, k].astype(F32)
    for copy in cf:
        copy.wait()
    for p in range(S):
        cgh_out[p // PS, other, p % PS] = zg2[p].astype(F32)


def shards(points, source, speed, live_count, index, fine_hidden, fine_edge, coarse_hidden,
           coarse_edge):
    S, B = lax.axis_size("sub"), lax.axis_size("blk")
    NP = points.shape[1]
    FD, H = fine_hidden.shape[0], fine_hidden.shape[1]
    CB = coarse_hidden.shape[0]
    C = CB * B
    PS = S // CB
    cap = index.shape[1]
    half = H // 2
    Q = half // B
    RP = half // PS
    wire = BF16 if RP % 16 == 0 else F32
    NE = FD + 5
    vm, dma = pltpu.VMEM, pltpu.SemaphoreType.DMA
    scratch = [
        vm((C, H, H), BF16), vm((C, 8, H), F32), vm((FD, 8, H), F32),
        vm((H, H), BF16), vm((H, H), BF16), vm((8, H), F32), vm((8, H), F32),
        vm((128, NP), F32), vm((NP, 128), F32), vm((128, 128), F32), vm((128, 128), F32),
        vm((NP, 128), F32), vm((128, NP), F32),
        vm((NP, 128), F32), vm((128, 128), F32), vm((NP, 128), F32), vm((128, 128), F32),
        vm((8, 128), jnp.int32),
        vm((FD + 3, 7, NP, H), BF16), vm((FD + 3, 7, NP, H), F32), vm((FD + 3, NP, H), F32),
        vm((2, 7, cap, H), BF16), vm((2, 7, cap, H), F32), vm((2, cap, H), F32),
        vm((7, NP, H), BF16),
        vm((NE, 2, B, Q, H), F32), vm((NE, B, Q, H), F32),
        vm((C, 8, H), F32), vm((C, 8, H), F32), vm((2, 8, H), F32), vm((2, 8, H), F32),
        vm((FD, 8, H), F32), vm((FD, 8, H), F32),
        vm((C, PS, RP, H), F32), vm((C, PS, RP, H), wire), vm((B, CB, PS, RP, H), wire),
        vm((CB, PS, RP, H), F32), vm((CB, PS, RP, H), wire), vm((S, RP, H), wire),
        vm((S, RP, H), wire), vm((S, RP, H), wire), vm((B, CB, 8, H), F32),
        vm((S, CB, 8, H), F32),
        vm((2 + FD, Q, H), F32), vm((B, 2 + FD, Q, H), BF16), vm((B, 2 + FD, Q, H), BF16),
        vm((2, Q, H), BF16), vm((2, Q, H), BF16), vm((B, 2, 8, H), F32), vm((2, 8, H), F32),
        vm((B, FD, 8, H), F32),
        vm((8, 128), F32), vm((B, FD, Q, H), BF16), vm((B, FD, Q, H), BF16),
        dma((4 + 2 * B,)), dma((4 + 2 * B,)), dma((NE + 3,)), dma((NE + 3,)),
        dma((B, 6)), dma((B, 6)), dma((S, 4)), dma((S, 4)),
        dma((4 + 2 * B,)), dma((4 + 2 * B,)),
    ]
    space = pl.BlockSpec(memory_space=pltpu.VMEM)
    outs = pl.pallas_call(
        functools.partial(kernel, S, B, CB, FD),
        out_shape=(
            jax.ShapeDtypeStruct((1, NP), F32),
            jax.ShapeDtypeStruct((FD, 2, B, Q, H), F32),
            jax.ShapeDtypeStruct((FD, 6, H), F32),
            jax.ShapeDtypeStruct((CB, 2, PS, RP, H), F32),
            jax.ShapeDtypeStruct((CB, 6, H), F32),
            jax.ShapeDtypeStruct((1, 128), F32),
        ),
        in_specs=[space] * 3 + [pl.BlockSpec(memory_space=pltpu.SMEM)] + [space] * 5,
        out_specs=(space,) * 6,
        scratch_shapes=scratch,
        compiler_params=pltpu.CompilerParams(
            collective_id=0, has_side_effects=True, vmem_limit_bytes=56 * 1024 * 1024
        ),
    )(
        points, source.reshape(1, NP), speed.reshape(1, NP), live_count, index,
        fine_hidden, fine_edge, coarse_hidden, coarse_edge,
    )
    return (
        outs[0].reshape(NP), outs[1].reshape(FD, H, H), outs[2], outs[3].reshape(CB, H, H),
        outs[4], outs[5][0, 0:1],
    )


def solution(mesh):
    return jax.shard_map(
        shards,
        mesh=mesh,
        in_specs=(
            P(None, ("groups", "sub", "blk", "rep")),
            P(("groups", "sub", "blk", "rep")),
            P(("groups", "sub", "blk", "rep")),
            P(("groups", "sub", "blk", "rep")),
            P(None, ("groups", "sub", "blk", "rep")),
            P("sub", None, None),
            P("sub", None, None),
            P("blk", None, None),
            P("blk", None, None),
        ),
        out_specs=(
            P(("groups", "sub", "blk", "rep")),
            P(("groups", "sub"), None, None),
            P(("groups", "sub"), None, None),
            P(("groups", "blk"), None, None),
            P(("groups", "blk"), None, None),
            P("groups"),
        ),
        check_vma=False,
    )
```

time: 240 us -> 53.9 us (0.22)
  blocking collectives: 82.1 us -> 0 us
  other arithmetic: 54.3 us -> 0 us
  Pallas kernels: 0 us -> 44.1 us
  local copies, waits for them, and re-layouts: 33.1 us -> 7.07 us
  matrix products: 21.1 us -> 0 us
  waiting for transfers between devices: 18.9 us -> 0 us
  between operations: 21.1 us -> 2.48 us
  starting transfers between devices: 7.24 us -> 0 us
    psum x3 -> x0, blocking collectives: 70 us -> none  [the longest x1 32.8 us: shards(): lax.psum((jnp.sum(residual * residual), live_count[0].astype(jnp.float32)...]
    pallas_call x0 -> x1, Pallas kernels: none -> 44.1 us  [shards(): pl.pallas_call(functools.partial(kernel, S, B, CB, FD), out_shape=(jax.Sh...]
    dot_general x24 -> x0, matrix products: 21.1 us -> none  [the longest x7 10.2 us: net_backward(): lax.dot_general(flat_streams, grad_low, (((0,), (0,)), ((), ())), preferr...]
    unnamed x420 -> x19, local copies, waits for them, and re-layouts: 27.4 us -> 7.07 us
    unnamed x31 -> x0, other arithmetic: 20.1 us -> none
    psum x2 -> x0, waiting for transfers between devices: 15.2 us -> none  [the longest x1 15.2 us: shards(): coarse_sums = lax.psum((owned[0], owned[1]), ('sub', 'rep'))]
    reduce_sum x22 -> x0, other arithmetic: 14.8 us -> none  [the longest x7 6.97 us: second_layer(): net_value = jnp.sum(active * weights_out, axis=-1)]
    all_gather x2 -> x0, blocking collectives: 12.2 us -> none  [the longest x1 7.82 us: shards(): lax.all_gather(coarse_hidden, 'blk', axis=0, tiled=True)]
  transfers between devices with their start and end apart: 8 -> 0, of which waited for: 2 -> 0; matrix products, arithmetic and copies ran while one was open for 31% -> 0% of each run, Pallas kernels for 0% -> 0%
where the time goes in v1:
time: 53.9 us; the launch traced here: 53.6 us
  Pallas kernels  44.1 us (82%)
  local copies, waits for them, and re-layouts  7.07 us (13%)
  between operations  2.48 us (5%)
    pallas_call x1, Pallas kernels, shards(): pl.pallas_call(functools.partial(kernel, S, B, CB, FD), out_shape=(jax.Sh...  44.1 us
    unnamed x19, local copies, waits for them, and re-layouts  7.07 us

profile of v1, /device:TPU:0, one launch (start us, length us, event | category | flops | bytes accessed | tf_op | source)
XLA Modules:
  0.0 53.6 jit_solution(15229355230794383616)
XLA Ops:
  1.3 0.0 copy-start.3
  1.3 1.3 %copy.15.fe_ref = bf16[2,6,256]{2,1,0:T(8,128)(2,1)} copy(bf16[2,6,256]{2,0,1:T(2,128)(2,1)} %param.15) | data formatting | bytes 12288 | tf_op args[6]
  2.6 0.0 copy-done.3
  2.6 0.6 %copy.16.ce_ref = bf16[2,6,256]{2,1,0:T(8,128)(2,1)} copy(bf16[2,6,256]{2,0,1:T(2,128)(2,1)S(1)} %copy-done.3) | data formatting | bytes 12288 | tf_op args[8]
  3.2 44.1 %shard_map.136 = (f32[1,128]{1,0:T(1,128)}, f32[2,2,2,64,256]{4,3,2,1,0:T(8,128)}, f32[2,6,256]{2,1,0:T(8,128)}, f32[2,2,2,64,256]{4,3,2,1,0:T(8,128)}, f32[2,6,256]{2,1,0:T(8,128)}, /*index=5*/f32[1,128]{1,0:T(1,128)}) custom-call(f32[3,128]{1,0:T(4,128)} %points_ref.1, f32[1,128]{1,0:T(1,128)} %bitcast.9, f32[1,128]{1,0:T(1,128)} %bitcast.10, ...), custom_call_target="tpu_custom_call" | custom-call | tf_op jit(solution)/shard_map/pallas_call | solution.py:591
  47.3 0.0 copy-start.2
  47.3 0.0 copy-start.1
  47.3 0.7 %copy-done.2 = f32[2,6,256]{2,1,0:T(8,128)S(1)} copy-done((f32[2,6,256]{2,1,0:T(8,128)S(1)}, f32[2,6,256]{2,1,0:T(8,128)}, u32[]{:S(2)}) %copy-start.2) | copy-done | bytes 12312
  48.0 0.6 %copy.17 = f32[2,6,256]{2,0,1:T(2,128)} copy(f32[2,6,256]{2,1,0:T(8,128)S(1)} %copy-done.2) | data formatting | bytes 24576
  48.6 0.0 copy-done.1
  48.6 0.0 copy-start.5
  48.6 0.6 %copy.18 = f32[2,6,256]{2,0,1:T(2,128)} copy(f32[2,6,256]{2,1,0:T(8,128)S(1)} %copy-done.1) | data formatting | bytes 24576
  49.2 0.0 copy-done.5
  49.2 0.5 copy.24
  49.7 0.0 copy-start
  49.7 1.9 %copy.25 = f32[2,256,256]{2,1,0:T(8,128)} copy(f32[2,256,256]{2,1,0:T(8,128)} %bitcast.8) | data formatting | bytes 1048576
  51.7 0.0 copy-done
  51.7 0.0 copy-start.4
  51.7 0.8 %copy.26 = f32[2,256,256]{2,1,0:T(8,128)} copy(f32[2,256,256]{2,1,0:T(8,128)S(1)} %bitcast.7) | data formatting | bytes 1048576
  52.5 0.0 copy-done.4
Async XLA Ops:
  1.3 1.3 %copy-start.3 = (bf16[2,6,256]{2,0,1:T(2,128)(2,1)S(1)}, bf16[2,6,256]{2,0,1:T(2,128)(2,1)}, u32[]{:S(2)}) copy-start(bf16[2,6,256]{2,0,1:T(2,128)(2,1)} %param.17) | copy-start | bytes 18436
  47.3 0.7 %copy-start.2 = (f32[2,6,256]{2,1,0:T(8,128)S(1)}, f32[2,6,256]{2,1,0:T(8,128)}, u32[]{:S(2)}) copy-start(f32[2,6,256]{2,1,0:T(8,128)} %get-tuple-element.20) | copy-start | bytes 36868
  47.3 1.3 %copy-start.1 = (f32[2,6,256]{2,1,0:T(8,128)S(1)}, f32[2,6,256]{2,1,0:T(8,128)}, u32[]{:S(2)}) copy-start(f32[2,6,256]{2,1,0:T(8,128)} %get-tuple-element.22) | copy-start | bytes 36868
  48.6 0.6 %copy-start.5 = (f32[1,128]{1,0:T(1,128)S(1)}, f32[1,128]{1,0:T(1,128)}, u32[]{:S(2)}) copy-start(f32[1,128]{1,0:T(1,128)} %get-tuple-element.12) | copy-start | bytes 1540
  49.7 1.9 %copy-start = (f32[2,2,2,64,256]{4,3,2,1,0:T(8,128)S(1)}, f32[2,2,2,64,256]{4,3,2,1,0:T(8,128)}, u32[]{:S(2)}) copy-start(f32[2,2,2,64,256]{4,3,2,1,0:T(8,128)} %get-tuple-element.15) | copy-start | bytes 1572868
  51.7 0.8 %copy-start.4 = (f32[1,128]{1,0:T(1,128)S(1)}, f32[1,128]{1,0:T(1,128)}, u32[]{:S(2)}) copy-start(f32[1,128]{1,0:T(1,128)} %get-tuple-element.17) | copy-start | bytes 1540

commit v2 on v1

v2 whole, which is shorter than its diff:
```python
import functools

import jax
import jax.numpy as jnp
from jax import lax
from jax.experimental import pallas as pl
from jax.experimental.pallas import tpu as pltpu
from jax.sharding import PartitionSpec as P

MESH = pl.DeviceIdType.MESH
F32 = jnp.float32
BF16 = jnp.bfloat16
WIDTH_SQ = 0.36
CHUNK = 16
UNROLL = 8
EXACT = lax.Precision.HIGHEST


def wide(tile, columns):
    return jnp.concatenate([tile] * (columns // tile.shape[1]), axis=1)


def fold(value):
    total = value[0:8]
    for at in range(8, value.shape[0], 8):
        total = total + value[at : at + 8]
    return total


def rows_of(step):
    return pl.ds(pl.multiple_of(step * CHUNK, CHUNK), CHUNK)


def window_rows(dx, width_sq, speed):
    weight = jnp.exp(-dx * dx / width_sq)
    weight_x = -2.0 * dx / width_sq * weight
    weight_xx = (4.0 * dx * dx / (width_sq * width_sq) - 2.0 / width_sq) * weight
    return (weight, speed * weight, 2.0 * speed * weight_x, speed * weight_xx)


class Net:
    def __init__(self, count, factors, edge, weights, cols, offset, ids, streams, layers, hidden):
        self.count, self.factors = count, factors
        self.edge, self.weights = edge, weights
        self.cols, self.offset, self.ids = cols, offset, ids
        self.streams, self.layers, self.hidden = streams, layers, hidden

    def col(self, name, step):
        at = self.ids[name]
        rows = pl.ds(pl.multiple_of(self.offset + step * CHUNK, CHUNK), CHUNK)
        return self.cols[rows, at : at + 1]

    def forward(self, totals):
        edge = self.edge()
        e = [edge[j : j + 1] for j in range(6)]
        columns = edge.shape[1]
        scaled = [self.factors[d] * e[d] for d in range(3)]
        squares = [s * s for s in scaled]

        def first(step, carry):
            rows = rows_of(step)
            pre = (
                self.col("t", step) * e[0]
                + self.col("x", step) * e[1]
                + self.col("y", step) * e[2]
                + e[3]
            )
            h = jnp.tanh(pre)
            g = 1.0 - h * h
            s = -2.0 * h * g
            self.hidden[rows, :] = h
            self.streams[0, rows, :] = h.astype(BF16)
            for d in range(3):
                self.streams[1 + d, rows, :] = (g * scaled[d]).astype(BF16)
                self.streams[4 + d, rows, :] = (s * squares[d]).astype(BF16)
            return carry

        steps = self.count // CHUNK
        lax.fori_loop(0, steps, first, 0, unroll=UNROLL)
        flat = self.streams[...].reshape(7 * self.count, columns)
        self.layers[...] = jnp.dot(
            flat, self.weights(), preferred_element_type=F32
        ).reshape(7, self.count, columns)
        out = e[5] * (1.0 / float(columns) ** 0.5)

        def second(step, carry):
            rows = rows_of(step)
            w, cw = self.col("w", step), self.col("cw", step)
            cx, cxx = self.col("cx", step), self.col("cxx", step)
            k = jnp.tanh(self.layers[0, rows, :] + e[4])
            m = 1.0 - k * k
            l1, l2, l3 = [self.layers[j, rows, :] for j in (1, 2, 3)]
            curved = (
                w * self.layers[4, rows, :]
                - cw * (self.layers[5, rows, :] + self.layers[6, rows, :])
                - cx * l2
            )
            q = w * (l1 * l1) - cw * (l2 * l2 + l3 * l3)
            v = curved - 2.0 * k * q
            t = m * v - cxx * k
            self.layers[0, rows, :] = k
            self.layers[4, rows, :] = v
            self.layers[5, rows, :] = q
            self.layers[6, rows, :] = t
            value = jnp.sum(t * out, axis=1, keepdims=True)
            at = pl.ds(pl.multiple_of(self.offset + step * CHUNK, CHUNK), CHUNK)
            totals[at, :] = totals[at, :] + jnp.broadcast_to(value, (CHUNK, 128))
            return carry

        lax.fori_loop(0, steps, second, 0, unroll=UNROLL)

    def backward(self, cotangent, grads, grad_out, edge_out):
        edge = self.edge()
        e = [edge[j : j + 1] for j in range(6)]
        columns = edge.shape[1]
        norm = 1.0 / float(columns) ** 0.5
        out = e[5] * norm
        scaled = [self.factors[d] * e[d] for d in range(3)]
        squares = [s * s for s in scaled]
        zero = jnp.zeros((8, columns), F32)
        steps = self.count // CHUNK
        low = grads.at[:, pl.ds(0, self.count), :]

        def first(step, carry):
            rows = rows_of(step)
            at = pl.ds(pl.multiple_of(self.offset + step * CHUNK, CHUNK), CHUNK)
            cot = wide(cotangent[at, :], columns)
            w, cw = self.col("w", step), self.col("cw", step)
            cx, cxx = self.col("cx", step), self.col("cxx", step)
            k, l1, l2, l3, v, q, t = [self.layers[j, rows, :] for j in range(7)]
            m = 1.0 - k * k
            com = cot * out * m
            k4 = 4.0 * k * com
            kc = k4 * cw
            g0 = com * (-2.0 * (k * v + m * q) - cxx)
            low[0, rows, :] = g0.astype(BF16)
            low[1, rows, :] = (-(k4 * w) * l1).astype(BF16)
            low[2, rows, :] = (kc * l2 - com * cx).astype(BF16)
            low[3, rows, :] = (kc * l3).astype(BF16)
            low[4, rows, :] = (com * w).astype(BF16)
            minus = (-(com * cw)).astype(BF16)
            low[5, rows, :] = minus
            low[6, rows, :] = minus
            return (carry[0] + fold(g0), carry[1] + fold(cot * t))

        sum4, sum5 = lax.fori_loop(0, steps, first, (zero, zero), unroll=UNROLL)
        flat = self.streams[...].reshape(7 * self.count, columns)
        flat_low = low[...].reshape(7 * self.count, columns)
        grad_out(
            lax.dot_general(
                flat, flat_low, (((0,), (0,)), ((), ())), preferred_element_type=F32
            )
        )
        self.layers[...] = lax.dot_general(
            flat_low, self.weights(), (((1,), (1,)), ((), ())), preferred_element_type=F32
        ).reshape(7, self.count, columns)

        def second(step, carry):
            rows = rows_of(step)
            h = self.hidden[rows, :]
            i = [self.layers[j, rows, :] for j in range(7)]
            h2 = h * h
            g = 1.0 - h2
            s = -2.0 * h * g
            lin = i[1] * scaled[0] + i[2] * scaled[1] + i[3] * scaled[2]
            quad = i[4] * squares[0] + i[5] * squares[1] + i[6] * squares[2]
            da = g * (i[0] - 2.0 * h * lin + (6.0 * h2 - 2.0) * quad)
            terms = [
                da,
                da * self.col("t", step),
                da * self.col("x", step),
                da * self.col("y", step),
            ]
            terms += [g * i[1 + d] for d in range(3)] + [s * i[4 + d] for d in range(3)]
            return tuple(c + fold(x) for c, x in zip(carry, terms))

        sums = lax.fori_loop(0, steps, second, (zero,) * 10, unroll=UNROLL)
        sums = [jnp.sum(x, axis=0, keepdims=True) for x in sums]
        rows = [
            sums[1 + d]
            + self.factors[d] * sums[4 + d]
            + 2.0 * self.factors[d] * scaled[d] * sums[7 + d]
            for d in range(3)
        ]
        rows.append(sums[0])
        rows.append(jnp.sum(sum4, axis=0, keepdims=True))
        rows.append(jnp.sum(sum5, axis=0, keepdims=True) * norm)
        for j, row in enumerate(rows):
            edge_out(j, row)


def row_tile(tile):
    return tile.T[0:8, :]


def column_tile(row):
    return jnp.broadcast_to(row, (row.shape[1], row.shape[1])).T


def kernel(
    S, B, CB, FD, points_ref, source_ref, speed_ref, live_ref, index_ref, fh_ref, fe_ref, ch_ref,
    ce_ref, res_out, fg, fge_out, zg, cge_out,
    cedge, fedge, rows_sc, cols, idx_sc, pick_t, pts, lsend, lrecv,
    totals, ltotals, cback, crecv, lback, lcr, cotr, cotc, lcots, lcotr, lcotc,
    st, layers, hid, stl, ll, hl, grads, gh, gr, cge, cge_r, fge, fge_r,
    csum, zst, zr, cez, fown, fst, fxr, fex,
    p_send, p_recv, chip_send, chip_recv, x_send, x_recv, z_send, z_recv, g_send, g_recv,
):
    C = CB * B
    PS = S // CB
    NP = points_ref.shape[1]
    cap = index_ref.shape[1]
    H = fh_ref.shape[1]
    s, b, r = lax.axis_index("sub"), lax.axis_index("blk"), lax.axis_index("rep")
    other = 1 - r
    right, left = lax.rem(s + 1, S), lax.rem(s + S - 1, S)
    peers = [lax.rem(b + d, B) for d in range(1, B)]
    cell = s // max(S // C, 1)
    half_width = float(FD * S) / float(C)
    start = s.astype(F32) * FD

    barrier = pltpu.get_barrier_semaphore()
    pl.semaphore_signal(barrier, inc=1, device_id={"rep": other}, device_id_type=MESH)
    for to in peers:
        pl.semaphore_signal(barrier, inc=1, device_id={"blk": to}, device_id_type=MESH)
    for d in range(1, S):
        pl.semaphore_signal(
            barrier, inc=1, device_id={"sub": lax.rem(s + d, S)}, device_id_type=MESH
        )

    fields = jnp.concatenate(
        [points_ref[...], speed_ref[...], jnp.zeros((4, NP), F32)], axis=0
    )
    pts[b] = fields
    x_rows = lax.broadcasted_iota(jnp.int32, (8, 128), 0) == 1
    idx_sc[...] = jnp.full_like(idx_sc, -1)
    for n in range(2):
        idx_sc[n : n + 1, 0:cap] = index_ref[n : n + 1, :]
        pick_t[n] = (
            lax.broadcasted_iota(jnp.int32, (NP, 128), 0) == idx_sc[n : n + 1, :]
        ).astype(F32)
        listed = jnp.dot(fields, pick_t[n], preferred_element_type=F32, precision=EXACT)
        centre = start - 0.5 if n == 0 else start + (FD + 0.5)
        lsend[n] = listed - jnp.where(x_rows, centre, 0.0)
    pl.semaphore_wait(barrier, S + B - 1)

    def remote(src, dst, send, recv, **where):
        copy = pltpu.make_async_remote_copy(
            src_ref=src, dst_ref=dst, send_sem=send, recv_sem=recv,
            device_id=where, device_id_type=MESH,
        )
        copy.start()
        return copy

    def to_sides(src, dst, at):
        return [
            remote(src.at[0], dst.at[1], p_send.at[at], p_recv.at[at], sub=left),
            remote(src.at[1], dst.at[0], p_send.at[at + 1], p_recv.at[at + 1], sub=right),
        ]

    def to_peers(src_at, dst, at):
        return [
            remote(src_at(to), dst.at[b], p_send.at[at + d], p_recv.at[at + d], blk=to)
            for d, to in enumerate(peers)
        ]

    lists_in = to_sides(lsend, lrecv, 0)
    points_in = to_peers(lambda to: pts.at[b], pts, 6)

    fine_edges = fe_ref[...].astype(F32)
    coarse_edges = ce_ref[...].astype(F32)
    for j in range(6):
        for k in range(FD):
            fedge[k, j : j + 1, :] = fine_edges[j][k : k + 1]
        for k in range(CB):
            cedge[k, j : j + 1, :] = coarse_edges[j][k : k + 1]

    fine_f = (2.0, 2.0, 2.0)
    coarse_f = (2.0, 2.0 / half_width, 2.0)

    def put(at, group):
        for j, row in enumerate(group):
            rows_sc[at + j : at + j + 1, :] = row
        return {"t": 0, "y": 1, "x": at, "w": at + 1, "cw": at + 2, "cx": at + 3, "cxx": at + 4}

    def time_and_y(block):
        rows_sc[0:1, :] = 2.0 * (block[0:1] - 0.5)
        rows_sc[1:2, :] = 2.0 * (block[2:3] - 0.5)

    def fine_rows(at, block, centre):
        dx = block[1:2] - centre
        return put(at, [2.0 * dx, *window_rows(dx, WIDTH_SQ, block[3:4])])

    def coarse_rows(at, block, k):
        shift = lax.rem(b * CB + k - cell + 1 + C, C)
        used = jnp.where(shift < 3, 1.0, 0.0).astype(F32)
        dx = block[1:2] - (cell.astype(F32) + (shift.astype(F32) - 0.5)) * half_width
        window = window_rows(dx, WIDTH_SQ * half_width * half_width, block[3:4])
        return put(at, [2.0 * dx / half_width, *(used * row for row in window)])

    rows_sc[...] = jnp.zeros_like(rows_sc)
    totals[...] = jnp.zeros_like(totals)
    ltotals[...] = jnp.zeros_like(ltotals)

    def coarse_net(place, k, ids):
        at = FD + place * CB + k
        return Net(NP, coarse_f, lambda: cedge[k], lambda: ch_ref[k], cols.at[place], 0, ids,
                   st.at[at], layers.at[at], hid.at[at])

    time_and_y(fields)
    fine_ids = [fine_rows(2 + 5 * k, fields, start + (k + 0.5)) for k in range(FD)]
    coarse_ids = [coarse_rows(2 + 5 * (FD + k), fields, k) for k in range(CB)]
    cols[0] = rows_sc[...].T
    fine = [
        Net(NP, fine_f, lambda k=k: fedge[k], lambda k=k: fh_ref[k], cols.at[0], 0,
            fine_ids[k], st.at[k], layers.at[k], hid.at[k])
        for k in range(FD)
    ]
    coarse = [[coarse_net(0, k, coarse_ids[k]) for k in range(CB)]]
    for net in fine:
        net.forward(totals.at[0])

    for copy in points_in:
        copy.wait()
    for d, source in enumerate(peers):
        block = pts[source]
        time_and_y(block)
        ids = [coarse_rows(2 + 5 * k, block, k) for k in range(CB)]
        cols[1 + d] = rows_sc[...].T
        nets = [coarse_net(1 + d, k, ids[k]) for k in range(CB)]
        coarse.append(nets)
        for net in nets:
            net.forward(totals.at[1 + d])
        cback[source] = row_tile(totals[1 + d])
    coarse_back = to_peers(lambda to: cback.at[to], crecv, 6 + B)

    for copy in lists_in:
        copy.wait()
    lists = []
    for n, k in ((0, 0), (1, FD - 1)):
        block = lrecv[n]
        time_and_y(block)
        ids = fine_rows(2, block, 0.0)
        cols[B + n] = rows_sc[...].T
        net = Net(cap, fine_f, lambda k=k: fedge[k], lambda k=k: fh_ref[k], cols.at[B + n], 0,
                  ids, stl.at[n], ll.at[n], hl.at[n])
        lists.append(net)
        net.forward(ltotals.at[n])
        lback[n] = row_tile(ltotals[n])
    lists_back = to_sides(lback, lcr, 2)

    for net in coarse[0]:
        net.forward(totals.at[0])
    total = row_tile(totals[0])
    for copy in coarse_back + lists_back:
        copy.wait()
    for source in peers:
        total = total + crecv[source]
    for n in range(2):
        total = total + lax.dot_general(
            lcr[n], pick_t[n], (((1,), (1,)), ((), ())), preferred_element_type=F32,
            precision=EXACT,
        )
    count = live_ref[0]
    live = (lax.broadcasted_iota(jnp.int32, (1, NP), 1) < count).astype(F32)
    residual = (total[0:1] * 0.125 - source_ref[...]) * live
    res_out[...] = residual
    cot = residual * 0.125
    loss = jnp.broadcast_to(jnp.sum(residual * residual, axis=1, keepdims=True), (1, NP))
    counted = jnp.full((1, NP), 1.0, F32) * count.astype(F32)
    cotr[b] = jnp.concatenate([cot, loss, counted, jnp.zeros((5, NP), F32)], axis=0)
    cot8 = jnp.broadcast_to(cot, (8, NP))
    for n in range(2):
        lcots[n] = jnp.dot(cot8, pick_t[n], preferred_element_type=F32, precision=EXACT)
    lists_cot = to_sides(lcots, lcotr, 4)
    peers_cot = to_peers(lambda to: cotr.at[b], cotr, 6 + 2 * B)
    cotc[0] = column_tile(cot)
    cge[...] = jnp.zeros_like(cge)
    fge[...] = jnp.zeros_like(fge)

    def run_back(e, net, cotangent, edge_ref, k, more):
        def keep(value):
            value = value.reshape(gh.shape[1:])
            gh[e] = gh[e] + value if more else value

        def keep_edge(j, row):
            edge_ref[k, j : j + 1, :] = edge_ref[k, j : j + 1, :] + row

        net.backward(cotangent, grads, keep, keep_edge)

    def to_core(e):
        return remote(gh.at[e, other], gr.at[e], chip_send.at[e], chip_recv.at[e], rep=other)

    NE = CB + FD
    chip = {}
    for k in range(CB):
        run_back(k, coarse[0][k], cotc.at[0], cge, k, False)
    for copy in peers_cot:
        copy.wait()
    for d, source in enumerate(peers):
        cotc[1 + d] = column_tile(cotr[source, 0:1, :])
    for k in range(CB):
        for d in range(B - 1):
            run_back(k, coarse[1 + d][k], cotc.at[1 + d], cge, k, True)
        chip[k] = to_core(k)
    sums = cotr[0]
    for q in range(1, B):
        sums = sums + cotr[q]
    cge[0, 6:8, :] = wide(sums[1:3], H)
    chip["ce"] = remote(cge, cge_r, chip_send.at[NE], chip_recv.at[NE], rep=other)

    run_back(CB, fine[0], cotc.at[0], fge, 0, False)

    cz = []
    for k in range(CB):
        chip[k].wait()
        value = (gh[k, r] + gr[k]).reshape(csum.shape[1:])
        csum[k] = value
        zst[k] = value.astype(zst.dtype)
    for d in range(1, S):
        to = lax.rem(s + d, S)
        cz.append(
            remote(zst.at[to // PS, lax.rem(to, PS)], zr.at[s], z_send.at[d, 0],
                   z_recv.at[d, 0], sub=to)
        )
    chip["ce"].wait()
    cez[s] = cge[...] + cge_r[...]
    for d in range(1, S):
        to = lax.rem(s + d, S)
        cz.append(remote(cez.at[s], cez.at[s], z_send.at[d, 1], z_recv.at[d, 1], sub=to))

    for k in range(1, FD):
        run_back(CB + k, fine[k], cotc.at[0], fge, k, False)
    for copy in lists_cot:
        copy.wait()
    for n, k in ((0, 0), (1, FD - 1)):
        lcotc[n] = column_tile(lcotr[n, 0:1, :])
        run_back(CB + k, lists[n], lcotc.at[n], fge, k, True)
    for k in range(FD):
        chip[CB + k] = to_core(CB + k)
    chip["fe"] = remote(fge, fge_r, chip_send.at[NE + 1], chip_recv.at[NE + 1], rep=other)

    fx = []
    for k in range(FD):
        chip[CB + k].wait()
        fown[k] = gh[CB + k, r, b] + gr[CB + k, b]
        for d, to in enumerate(peers):
            fst[to, k] = (gh[CB + k, r, to] + gr[CB + k, to]).astype(BF16)
    for d, to in enumerate(peers):
        fx.append(remote(fst.at[to], fxr.at[b], x_send.at[d, 0], x_recv.at[d, 0], blk=to))
    chip["fe"].wait()
    fex[b] = fge[...] + fge_r[...]
    for d, to in enumerate(peers):
        fx.append(remote(fex.at[b], fex.at[b], x_send.at[d, 1], x_recv.at[d, 1], blk=to))

    for copy in cz:
        copy.wait()
    piece = csum[s // PS, lax.rem(s, PS)]
    for d in range(1, S):
        piece = piece + zr[lax.rem(s + d, S)].astype(F32)
    zg[r, s] = piece.astype(zg.dtype)
    cg = []
    for d in range(1, S):
        to = lax.rem(s + d, S)
        cg.append(remote(zg.at[r, s], zg.at[r, s], z_send.at[d, 2], z_recv.at[d, 2], sub=to))
    last = [remote(zg.at[r, s], zg.at[r, s], z_send.at[0, 0], z_recv.at[0, 0], rep=other)]
    edge_sum = cez[0]
    for d in range(1, S):
        edge_sum = edge_sum + cez[d]
    cge_out[...] = edge_sum

    for copy in fx:
        copy.wait()
    for k in range(FD):
        value = fown[k]
        for source in peers:
            value = value + fxr[source, k].astype(F32)
        fg[r, b, k] = value.astype(BF16)
    fgc = [
        remote(fg.at[r, b], fg.at[r, b], g_send.at[1 + d], g_recv.at[1 + d], blk=to)
        for d, to in enumerate(peers)
    ]
    last.append(remote(fg.at[r, b], fg.at[r, b], g_send.at[0], g_recv.at[0], rep=other))
    edge_sum = fex[0]
    for q in range(1, B):
        edge_sum = edge_sum + fex[q]
    fge_out[...] = edge_sum

    for d in range(B - 1):
        fgc[d].wait()
        source = lax.rem(b + B - 1 - d, B)
        last.append(
            remote(fg.at[r, source], fg.at[r, source], g_send.at[B + d], g_recv.at[B + d],
                   rep=other)
        )
    for d in range(1, S):
        cg[d - 1].wait()
        source = lax.rem(s + S - d, S)
        last.append(
            remote(zg.at[r, source], zg.at[r, source], z_send.at[d, 3], z_recv.at[d, 3],
                   rep=other)
        )
    for copy in last:
        copy.wait()


def finish(res_in, fg, fe, zg, ce, res_out, fgh_out, fge_out, cgh_out, cge_out, loss_out):
    B, FD = fg.shape[1], fg.shape[2]
    S, CB = zg.shape[1], ce.shape[0]
    PS = S // CB
    res_out[...] = res_in[...]
    for half in range(2):
        for q in range(B):
            for k in range(FD):
                fgh_out[k, half, q] = fg[half, q, k].astype(F32)
        for p in range(S):
            cgh_out[p // PS, half, p % PS] = zg[half, p].astype(F32)
    for j in range(6):
        for k in range(FD):
            fge_out[j, k : k + 1, :] = fe[k, j : j + 1, :]
        for k in range(CB):
            cge_out[j, k : k + 1, :] = ce[k, j : j + 1, :]
    loss = ce[0, 6:7, 0:128] / ce[0, 7:8, 0:128]
    loss_out[0] = loss[0, 0]


def shards(points, source, speed, live_count, index, fine_hidden, fine_edge, coarse_hidden,
           coarse_edge):
    S, B = lax.axis_size("sub"), lax.axis_size("blk")
    NP = points.shape[1]
    FD, H = fine_hidden.shape[0], fine_hidden.shape[1]
    CB = coarse_hidden.shape[0]
    PS = S // CB
    cap = index.shape[1]
    half = H // 2
    Q = half // B
    RP = half // PS
    wire = BF16 if RP % 16 == 0 else F32
    NE = FD + CB
    NN = FD + B * CB
    vm, dma = pltpu.VMEM, pltpu.SemaphoreType.DMA
    scratch = [
        vm((CB, 8, H), F32), vm((FD, 8, H), F32), vm((128, NP), F32), vm((B + 2, NP, 128), F32),
        vm((8, 128), jnp.int32), vm((2, NP, 128), F32), vm((B, 8, NP), F32),
        vm((2, 8, 128), F32), vm((2, 8, 128), F32),
        vm((B, NP, 128), F32), vm((2, NP, 128), F32), vm((B, 8, NP), F32), vm((B, 8, NP), F32),
        vm((2, 8, NP), F32), vm((2, 8, NP), F32), vm((B, 8, NP), F32), vm((B, NP, 128), F32),
        vm((2, 8, 128), F32), vm((2, 8, 128), F32), vm((2, NP, 128), F32),
        vm((NN, 7, NP, H), BF16), vm((NN, 7, NP, H), F32), vm((NN, NP, H), F32),
        vm((2, 7, cap, H), BF16), vm((2, 7, cap, H), F32), vm((2, cap, H), F32),
        vm((7, NP, H), BF16),
        vm((NE, 2, B, Q, H), F32), vm((NE, B, Q, H), F32),
        vm((CB, 8, H), F32), vm((CB, 8, H), F32), vm((FD, 8, H), F32), vm((FD, 8, H), F32),
        vm((CB, PS, RP, H), F32), vm((CB, PS, RP, H), wire), vm((S, RP, H), wire),
        vm((S, CB, 8, H), F32),
        vm((FD, Q, H), F32), vm((B, FD, Q, H), BF16), vm((B, FD, Q, H), BF16),
        vm((B, FD, 8, H), F32),
        dma((6 + 3 * B,)), dma((6 + 3 * B,)), dma((NE + 2,)), dma((NE + 2,)),
        dma((B, 2)), dma((B, 2)), dma((S, 4)), dma((S, 4)), dma((2 * B,)), dma((2 * B,)),
    ]
    space = pl.BlockSpec(memory_space=pltpu.VMEM)
    scalar = pl.BlockSpec(memory_space=pltpu.SMEM)
    shape = jax.ShapeDtypeStruct
    parts = pl.pallas_call(
        functools.partial(kernel, S, B, CB, FD),
        out_shape=(
            shape((1, NP), F32),
            shape((2, B, FD, Q, H), BF16),
            shape((FD, 8, H), F32),
            shape((2, S, RP, H), wire),
            shape((CB, 8, H), F32),
        ),
        in_specs=[space] * 3 + [scalar] + [space] * 5,
        out_specs=(space,) * 5,
        scratch_shapes=scratch,
        compiler_params=pltpu.CompilerParams(
            collective_id=0, has_side_effects=True, vmem_limit_bytes=56 * 1024 * 1024
        ),
    )(
        points, source.reshape(1, NP), speed.reshape(1, NP), live_count, index,
        fine_hidden, fine_edge.transpose(1, 0, 2), coarse_hidden, coarse_edge.transpose(1, 0, 2),
    )
    outs = pl.pallas_call(
        finish,
        out_shape=(
            shape((1, NP), F32),
            shape((FD, 2, B, Q, H), F32),
            shape((6, FD, H), F32),
            shape((CB, 2, PS, RP, H), F32),
            shape((6, CB, H), F32),
            shape((1,), F32),
        ),
        in_specs=[space] * 5,
        out_specs=(space,) * 5 + (scalar,),
        compiler_params=pltpu.CompilerParams(vmem_limit_bytes=32 * 1024 * 1024),
    )(*parts)
    return (
        outs[0].reshape(NP), outs[1].reshape(FD, H, H), outs[2].transpose(1, 0, 2),
        outs[3].reshape(CB, H, H), outs[4].transpose(1, 0, 2), outs[5],
    )


def solution(mesh):
    return jax.shard_map(
        shards,
        mesh=mesh,
        in_specs=(
            P(None, ("groups", "sub", "blk", "rep")),
            P(("groups", "sub", "blk", "rep")),
            P(("groups", "sub", "blk", "rep")),
            P(("groups", "sub", "blk", "rep")),
            P(None, ("groups", "sub", "blk", "rep")),
            P("sub", None, None),
            P("sub", None, None),
            P("blk", None, None),
            P("blk", None, None),
        ),
        out_specs=(
            P(("groups", "sub", "blk", "rep")),
            P(("groups", "sub"), None, None),
            P(("groups", "sub"), None, None),
            P(("groups", "blk"), None, None),
            P(("groups", "blk"), None, None),
            P("groups"),
        ),
        check_vma=False,
    )
```

time: 53.9 us -> 40.6 us (0.75)
  Pallas kernels: 44.1 us -> 35 us
  local copies, waits for them, and re-layouts: 7.07 us -> 3.98 us
  between operations: 2.48 us -> 1.3 us
    pallas_call x1 -> x2, Pallas kernels: 44.1 us -> 35 us  [the longest x1 34 us: shards(): pl.pallas_call(functools.partial(kernel, S, B, CB, FD), out_shape=(shape(...]
    unnamed x19 -> x10, local copies, waits for them, and re-layouts: 7.07 us -> 3.98 us
where the time goes in v2:
time: 40.6 us; the launch traced here: 40.3 us
  Pallas kernels  35 us (86%)
  local copies, waits for them, and re-layouts  3.98 us (10%)
  between operations  1.3 us (3%)
    pallas_call x1, Pallas kernels, shards(): pl.pallas_call(functools.partial(kernel, S, B, CB, FD), out_shape=(shape(...  34 us
    unnamed x10, local copies, waits for them, and re-layouts  3.98 us
    pallas_call x1, Pallas kernels, shards(): pl.pallas_call(finish, out_shape=(shape((1, NP), F32), shape((FD, 2, B, Q...  1.03 us

profile of v2, /device:TPU:0, one launch (start us, length us, event | category | flops | bytes accessed | tf_op | source)
XLA Modules:
  0.0 40.3 jit_solution(13725845390796742996)
XLA Ops:
  1.3 34.0 %shard_map.136 = (f32[1,128]{1,0:T(1,128)}, bf16[2,2,2,64,256]{4,3,2,1,0:T(8,128)(2,1)}, f32[2,8,256]{2,1,0:T(8,128)}, bf16[2,4,64,256]{3,2,1,0:T(8,128)(2,1)}, f32[2,8,256]{2,1,0:T(8,128)}) custom-call(f32[3,128]{1,0:T(4,128)} %points_ref.1, f32[1,128]{1,0:T(1,128)} %bitcast.11, f32[1,128]{1,0:T(1,128)} %bitcast.12, s32[1]{0:T(128)S(6)} %copy.15.live_ref, ...), custom_call_target="tpu_custom_call" | custom-call | tf_op jit(solution)/shard_map/pallas_call | solution.py:564
  35.3 0.0 copy-start.4
  35.3 0.6 %copy-done.4 = f32[1,128]{1,0:T(1,128)S(1)} copy-done((f32[1,128]{1,0:T(1,128)S(1)}, f32[1,128]{1,0:T(1,128)}, u32[]{:S(2)}) %copy-start.4) | copy-done | bytes 536
  35.9 0.0 copy-start
  35.9 0.9 %copy-done = bf16[2,2,2,64,256]{4,3,2,1,0:T(8,128)(2,1)S(1)} copy-done((bf16[2,2,2,64,256]{4,3,2,1,0:T(8,128)(2,1)S(1)}, bf16[2,2,2,64,256]{4,3,2,1,0:T(8,128)(2,1)}, u32[]{:S(2)}) %copy-start) | copy-done | bytes 262168
  36.9 0.0 copy-start.1
  36.9 0.9 %copy-done.1 = bf16[2,4,64,256]{3,2,1,0:T(8,128)(2,1)S(1)} copy-done((bf16[2,4,64,256]{3,2,1,0:T(8,128)(2,1)S(1)}, bf16[2,4,64,256]{3,2,1,0:T(8,128)(2,1)}, u32[]{:S(2)}) %copy-start.1) | copy-done | bytes 262168
  37.8 0.0 copy-start.2
  37.8 0.7 %copy-done.2 = f32[2,8,256]{2,1,0:T(8,128)S(1)} copy-done((f32[2,8,256]{2,1,0:T(8,128)S(1)}, f32[2,8,256]{2,1,0:T(8,128)}, u32[]{:S(2)}) %copy-start.2) | copy-done | bytes 16408
  38.5 0.0 copy-start.3
  38.5 0.7 %copy-done.3 = f32[2,8,256]{2,1,0:T(8,128)S(1)} copy-done((f32[2,8,256]{2,1,0:T(8,128)S(1)}, f32[2,8,256]{2,1,0:T(8,128)}, u32[]{:S(2)}) %copy-start.3) | copy-done | bytes 16408
  39.2 1.0 %shard_map.137 = (f32[1,128]{1,0:T(1,128)}, f32[2,2,2,64,256]{4,3,2,1,0:T(8,128)}, f32[6,2,256]{2,1,0:T(2,128)}, f32[2,2,2,64,256]{4,3,2,1,0:T(8,128)}, f32[6,2,256]{2,1,0:T(2,128)}, /*index=5*/f32[1]{0:T(128)}) custom-call(f32[1,128]{1,0:T(1,128)S(1)} %copy-done.4, bf16[2,2,2,64,256]{4,3,2,1,0:T(8,128)(2,1)S(1)} %copy-done, f32[2,8,256]{2,1,0:T(8,128)S(1)} %copy-done.2, ...), custom_call_target="tpu_custom_call" | custom-call | tf_op jit(solution)/shard_map/pallas_call | solution.py:583
Async XLA Ops:
  35.3 0.7 %copy-start.4 = (f32[1,128]{1,0:T(1,128)S(1)}, f32[1,128]{1,0:T(1,128)}, u32[]{:S(2)}) copy-start(f32[1,128]{1,0:T(1,128)} %get-tuple-element.17.res_in) | copy-start | bytes 1540
  35.9 0.9 %copy-start = (bf16[2,2,2,64,256]{4,3,2,1,0:T(8,128)(2,1)S(1)}, bf16[2,2,2,64,256]{4,3,2,1,0:T(8,128)(2,1)}, u32[]{:S(2)}) copy-start(bf16[2,2,2,64,256]{4,3,2,1,0:T(8,128)(2,1)} %get-tuple-element.18.fg) | copy-start | bytes 786436
  36.9 0.9 %copy-start.1 = (bf16[2,4,64,256]{3,2,1,0:T(8,128)(2,1)S(1)}, bf16[2,4,64,256]{3,2,1,0:T(8,128)(2,1)}, u32[]{:S(2)}) copy-start(bf16[2,4,64,256]{3,2,1,0:T(8,128)(2,1)} %get-tuple-element.20.zg) | copy-start | bytes 786436
  37.8 0.7 %copy-start.2 = (f32[2,8,256]{2,1,0:T(8,128)S(1)}, f32[2,8,256]{2,1,0:T(8,128)}, u32[]{:S(2)}) copy-start(f32[2,8,256]{2,1,0:T(8,128)} %get-tuple-element.19.fe) | copy-start | bytes 49156
  38.5 0.7 %copy-start.3 = (f32[2,8,256]{2,1,0:T(8,128)S(1)}, f32[2,8,256]{2,1,0:T(8,128)}, u32[]{:S(2)}) copy-start(f32[2,8,256]{2,1,0:T(8,128)} %get-tuple-element.21.ce) | copy-start | bytes 49156

commit v3 on v2

--- a/solution.py
+++ b/solution.py
@@ -592,7 +592,7 @@
         ),
         in_specs=[space] * 5,
         out_specs=(space,) * 5 + (scalar,),
-        compiler_params=pltpu.CompilerParams(vmem_limit_bytes=32 * 1024 * 1024),
+        compiler_params=pltpu.CompilerParams(vmem_limit_bytes=60 * 1024 * 1024),
     )(*parts)
     return (
         outs[0].reshape(NP), outs[1].reshape(FD, H, H), outs[2].transpose(1, 0, 2),

time: 40.6 us -> 37.5 us (0.924)
  local copies, waits for them, and re-layouts: 3.98 us -> 0 us
  Pallas kernels: 35 us -> 36 us
    unnamed x10 -> x0, local copies, waits for them, and re-layouts: 3.98 us -> none
    pallas_call x1, Pallas kernels: 1.03 us -> 2.07 us  [shards(): pl.pallas_call(finish, out_shape=(shape((1, NP), F32), shape((FD, 2, B, Q...]
where the time goes in v3:
time: 37.5 us; the launch traced here: 37.3 us
  Pallas kernels  36 us (96%)
  between operations  1.29 us (3%)
    pallas_call x1, Pallas kernels, shards(): pl.pallas_call(functools.partial(kernel, S, B, CB, FD), out_shape=(shape(...  33.9 us
    pallas_call x1, Pallas kernels, shards(): pl.pallas_call(finish, out_shape=(shape((1, NP), F32), shape((FD, 2, B, Q...  2.07 us

profile of v3, /device:TPU:0, one launch (start us, length us, event | category | flops | bytes accessed | tf_op | source)
XLA Modules:
  0.0 37.3 jit_solution(13295788020630183272)
XLA Ops:
  1.3 33.9 %shard_map.136 = (f32[1,128]{1,0:T(1,128)}, bf16[2,2,2,64,256]{4,3,2,1,0:T(8,128)(2,1)}, f32[2,8,256]{2,1,0:T(8,128)}, bf16[2,4,64,256]{3,2,1,0:T(8,128)(2,1)}, f32[2,8,256]{2,1,0:T(8,128)}) custom-call(f32[3,128]{1,0:T(4,128)} %points_ref.1, f32[1,128]{1,0:T(1,128)} %bitcast.11, f32[1,128]{1,0:T(1,128)} %bitcast.12, s32[1]{0:T(128)S(6)} %copy.15.live_ref, ...), custom_call_target="tpu_custom_call" | custom-call | tf_op jit(solution)/shard_map/pallas_call | solution.py:564
  35.2 2.1 %shard_map.137 = (f32[1,128]{1,0:T(1,128)}, f32[2,2,2,64,256]{4,3,2,1,0:T(8,128)}, f32[6,2,256]{2,1,0:T(2,128)}, f32[2,2,2,64,256]{4,3,2,1,0:T(8,128)}, f32[6,2,256]{2,1,0:T(2,128)}, /*index=5*/f32[1]{0:T(128)}) custom-call(f32[1,128]{1,0:T(1,128)} %get-tuple-element.17.res_in, bf16[2,2,2,64,256]{4,3,2,1,0:T(8,128)(2,1)} %get-tuple-element.18.fg, ...), custom_call_target="tpu_custom_call" | custom-call | tf_op jit(solution)/shard_map/pallas_call | solution.py:583
